TPU v7x, 32 devices: a whole 2x2x4 slice. The times are simulated.
32 devices in a mesh: tok: 8 (over z, core), wid: 4 (over y, x).
Axes of the slice: x: 2, y: 2, z: 4, core: 2. Of those that a mesh axis runs over, the one named last changes fastest.
Arguments:
- hidden: bfloat16 [4224, 1280], P('tok', 'wid'), may hold values from -30 to 30
- w_qkv: bfloat16 [1280, 1920], P('tok', 'wid'), may hold values from -0.15625 to 0.15625
- w_out: bfloat16 [1280, 1280], P('tok', 'wid'), may hold values from -0.15625 to 0.15625
- w_gate: bfloat16 [1280, 3584], P('tok', 'wid'), may hold values from -0.15625 to 0.15625
- w_up: bfloat16 [1280, 3584], P('tok', 'wid'), may hold values from -0.15625 to 0.15625
- w_down: bfloat16 [3584, 1280], P('wid', 'tok'), may hold values from -0.125 to 0.125
- g_attn: float32 [1280], replicated, may hold values from 0.1 to 1.9
- g_ffn: float32 [1280], replicated, may hold values from 0.1 to 1.9
- lengths: int32 [136], P('tok'), may hold values from 0 to 2048, as said below
- k_cache: bfloat16 [136, 2048, 320], P('tok', 'wid'), may hold values from -45 to 45
- v_cache: bfloat16 [136, 2048, 320], P('tok', 'wid'), may hold values from -4 to 4
Outputs:
- output: bfloat16 [4224, 1280], P('tok', 'wid')
- new_kv: bfloat16 [4224, 640], P('tok', 'wid')
Inputs may be any that keep to these rules, and one draw needn't show every extreme that they name: `lengths`: each request's entry is at most 2048, and some request has exactly 2048.
All inputs are finite; a program needn't handle non-finite values.
Results may differ from a plain program's by a relative error of at most 0.017.
Values may be sent and summed in bfloat16 or wider, within the bound.
A program may use at most 128 MiB of HBM per device.

v0:
```python
import jax
import jax.numpy as jnp
from jax import lax
from jax.sharding import PartitionSpec as P

HEADS = 20
KV_HEADS = 5
HEAD_DIM = 64
STRETCH = 512


EPSILON = 1e-05
MASKED = -1e30
SCORE_SCALE = 0.125


def norm_rows(values, gain):
    wide = values.astype(jnp.float32)
    mean_square = jnp.mean(wide * wide, axis=-1, keepdims=True)
    return (wide * lax.rsqrt(mean_square + EPSILON) * gain).astype(jnp.bfloat16)


def rotate(parts, places):
    half = parts.shape[-1] // 2
    ladder = jnp.arange(half).astype(jnp.float32) * (2.0 / parts.shape[-1])
    freqs = jnp.power(10000.0, -ladder)
    angles = places.astype(jnp.float32)[:, None] * freqs[None, :]
    cosine = jnp.cos(angles)[:, None, :]
    sine = jnp.sin(angles)[:, None, :]
    first = parts[..., :half]
    second = parts[..., half:]
    return jnp.concatenate(
        [first * cosine - second * sine, second * cosine + first * sine], axis=-1
    )


def shards(hidden, w_qkv, w_out, w_gate, w_up, w_down, g_attn, g_ffn, lengths, k_cache, v_cache):
    wid_count = lax.axis_size("wid")
    wid_place = lax.axis_index("wid")
    row_count = hidden.shape[0]
    query_width = HEADS * HEAD_DIM
    kv_width = KV_HEADS * HEAD_DIM
    groups = HEADS // KV_HEADS
    full_rows = lax.all_gather(hidden, "wid", axis=1, tiled=True)
    normed = norm_rows(full_rows, g_attn)
    tall_cols = lax.all_gather(w_qkv, "tok", axis=0, tiled=True)
    own_cols = jnp.dot(normed, tall_cols, preferred_element_type=jnp.float32)
    mixed = lax.all_gather(own_cols.astype(jnp.bfloat16), "wid", axis=1, tiled=True)
    stretch_rows = lengths[0] + jnp.arange(STRETCH)
    places = jnp.concatenate([stretch_rows, lengths[1:]])
    query = rotate(
        mixed[:, :query_width].astype(jnp.float32).reshape(row_count, HEADS, HEAD_DIM), places
    ).astype(jnp.bfloat16)
    keys = rotate(
        mixed[:, query_width : query_width + kv_width]
        .astype(jnp.float32)
        .reshape(row_count, KV_HEADS, HEAD_DIM),
        places,
    ).astype(jnp.bfloat16)
    values = mixed[:, query_width + kv_width :]
    new_kv_all = jnp.concatenate([keys.reshape(row_count, kv_width), values], axis=1)
    kv_share = 2 * kv_width // wid_count
    new_kv = lax.dynamic_slice_in_dim(new_kv_all, wid_place * kv_share, kv_share, 1)
    value_heads = values.reshape(row_count, KV_HEADS, HEAD_DIM)
    span = k_cache.shape[1]
    requests = k_cache.shape[0]
    query_heads = query.reshape(row_count, KV_HEADS, groups, HEAD_DIM)
    old_keys = k_cache.reshape(requests, span, KV_HEADS, HEAD_DIM)
    old_values = v_cache.reshape(requests, span, KV_HEADS, HEAD_DIM)
    spots = wid_place * span + jnp.arange(span)
    live = spots[None, :] < lengths[:, None]
    score_stretch = (
        jnp.einsum(
            "rkgd,pkd->rkgp", query_heads[:STRETCH], old_keys[0], preferred_element_type=jnp.float32
        )
        * SCORE_SCALE
    )
    score_stretch = jnp.where(live[0][None, None, None, :], score_stretch, MASKED)
    score_decode = (
        jnp.einsum(
            "jkgd,jpkd->jkgp",
            query_heads[STRETCH:],
            old_keys[1:],
            preferred_element_type=jnp.float32,
        )
        * SCORE_SCALE
    )
    score_decode = jnp.where(live[1:][:, None, None, :], score_decode, MASKED)
    band = row_count // wid_count
    first_row = wid_place * band
    query_mine = lax.dynamic_slice_in_dim(query_heads, first_row, band, 0)
    later = first_row + jnp.arange(band)[:, None]
    earlier = jnp.arange(row_count)[None, :]
    fresh_ok = (later < STRETCH) & (earlier < STRETCH) & (earlier <= later) | (later >= STRETCH) & (
        earlier == later
    )
    score_fresh = (
        jnp.einsum("rkgd,jkd->rkgj", query_mine, keys, preferred_element_type=jnp.float32)
        * SCORE_SCALE
    )
    score_fresh = jnp.where(fresh_ok[:, None, None, :], score_fresh, MASKED)
    cache_peak = jnp.concatenate([score_stretch.max(-1), score_decode.max(-1)], axis=0)
    fresh_peak = lax.dynamic_update_slice_in_dim(
        jnp.full(cache_peak.shape, MASKED, jnp.float32), score_fresh.max(-1), first_row, 0
    )
    peak = lax.pmax(jnp.maximum(cache_peak, fresh_peak).astype(jnp.bfloat16), "wid").astype(
        jnp.float32
    )
    expo_stretch = jnp.exp(score_stretch - peak[:STRETCH, :, :, None])
    expo_decode = jnp.exp(score_decode - peak[STRETCH:, :, :, None])
    peak_mine = lax.dynamic_slice_in_dim(peak, first_row, band, 0)
    expo_fresh = jnp.exp(score_fresh - peak_mine[:, :, :, None])
    totals = jnp.concatenate([expo_stretch.sum(-1), expo_decode.sum(-1)], axis=0)
    sums = jnp.concatenate(
        [
            jnp.einsum(
                "rkgp,pkd->rkgd",
                expo_stretch.astype(jnp.bfloat16),
                old_values[0],
                preferred_element_type=jnp.float32,
            ),
            jnp.einsum(
                "jkgp,jpkd->jkgd",
                expo_decode.astype(jnp.bfloat16),
                old_values[1:],
                preferred_element_type=jnp.float32,
            ),
        ],
        axis=0,
    )
    fresh_sums = jnp.einsum(
        "rkgj,jkd->rkgd",
        expo_fresh.astype(jnp.bfloat16),
        value_heads,
        preferred_element_type=jnp.float32,
    )
    sums = lax.dynamic_update_slice_in_dim(
        sums, lax.dynamic_slice_in_dim(sums, first_row, band, 0) + fresh_sums, first_row, 0
    )
    totals = lax.dynamic_update_slice_in_dim(
        totals,
        lax.dynamic_slice_in_dim(totals, first_row, band, 0) + expo_fresh.sum(-1),
        first_row,
        0,
    )
    sums_all, totals_all = (
        lax.psum(sums.reshape(row_count, query_width).astype(jnp.bfloat16), "wid").astype(
            jnp.float32
        ),
        lax.psum(totals.reshape(row_count, HEADS).astype(jnp.bfloat16), "wid").astype(jnp.float32),
    )
    merged = sums_all.reshape(row_count, HEADS, HEAD_DIM) / totals_all[:, :, None]
    attended = merged.astype(jnp.bfloat16).reshape(row_count, query_width)
    out_whole = lax.all_gather(w_out, "tok", axis=0, tiled=True)
    projected = jnp.dot(attended, out_whole, preferred_element_type=jnp.float32)
    residual = hidden.astype(jnp.float32) + projected
    middle = residual.astype(jnp.bfloat16)
    middle_full = lax.all_gather(middle, "wid", axis=1, tiled=True)
    normed_ffn = norm_rows(middle_full, g_ffn)
    gate_whole, up_whole = (
        lax.all_gather(w_gate, "tok", axis=0, tiled=True),
        lax.all_gather(w_up, "tok", axis=0, tiled=True),
    )
    gate = jnp.dot(normed_ffn, gate_whole, preferred_element_type=jnp.float32)
    up = jnp.dot(normed_ffn, up_whole, preferred_element_type=jnp.float32)
    activated = (jax.nn.silu(gate) * up).astype(jnp.bfloat16)
    down_full = lax.all_gather(w_down, "tok", axis=1, tiled=True)
    own_sums = lax.psum_scatter(
        lax.dot_general(
            down_full, activated, (((0,), (1,)), ((), ())), preferred_element_type=jnp.float32
        ).astype(jnp.bfloat16),
        "wid",
        scatter_dimension=0,
        tiled=True,
    ).astype(jnp.float32)
    output = (residual + own_sums.T).astype(jnp.bfloat16)
    return (output, new_kv)


def solution(mesh):
    placed = (
        P("tok", "wid"),
        P("tok", "wid"),
        P("tok", "wid"),
        P("tok", "wid"),
        P("tok", "wid"),
        P("wid", "tok"),
        P(),
        P(),
        P("tok"),
        P("tok", "wid", None),
        P("tok", "wid", None),
    )
    return jax.shard_map(
        shards,
        mesh=mesh,
        in_specs=placed,
        out_specs=(P("tok", "wid"), P("tok", "wid")),
        check_vma=False,
    )
```

profile of v0, /device:TPU:0, one launch (start us, length us, event | category | flops | bytes accessed | tf_op | source)
XLA Modules:
  0.0 439.3 jit_solution(17540917299224377007)
XLA Ops:
  7.2 0.7 all-gather.19.cloned.1.call-update
  7.9 0.7 all-gather.11.cloned.1.call-update
  8.7 35.3 %all-gather.19.cloned.1.call-done = bf16[4,320,528]{1,2,0:T(8,128)(2,1)} async-done(((bf16[1,320,528]{1,2,0:T(8,128)(2,1)}), bf16[4,320,528]{1,2,0:T(8,128)(2,1)}) %all-gather.19.cloned.1.call-update) | async-done | bytes 1351696 | tf_op jit(solution)/shard_map/all_gather | solution.py:44
  44.0 2.0 copy.48
  46.0 3.0 reshape.243
  49.0 2.2 multiply_reduce_fusion.1
  51.2 17.8 %all-gather.11.cloned.1.call-done = bf16[1280,480]{1,0:T(8,128)(2,1)} async-done(((bf16[160,480]{1,0:T(8,128)(2,1)}), bf16[1280,480]{1,0:T(8,128)(2,1)}) %all-gather.11.cloned.1.call-update) | async-done | bytes 1228816 | tf_op jit(solution)/shard_map/all_gather | solution.py:46
  69.1 3.1 fusion.30
  72.3 5.4 %slice.83 = bf16[16,512,320]{1,2,0:T(8,128)(2,1)} slice(bf16[17,512,320]{1,2,0:T(8,128)(2,1)} %param.20), slice={[1:17], [0:512], [0:320]} | slice | bytes 10485760 | tf_op jit(solution)/shard_map/slice | solution.py:83
  77.7 2.8 slice.91
  80.9 0.8 fusion.39
  81.7 0.4 multiply_cosine_fusion
  82.1 17.6 %all_gather.27 = bf16[1280,320]{1,0:T(8,128)(2,1)} all-gather(bf16[160,320]{1,0:T(8,128)(2,1)S(1)} %copy-done.20), channel_id=1, replica_groups=mesh['tok'=8,'wid'=4] {'tok'}, dimensions={0}, use_global_device_ids=true | all-gather | bytes 921600 | tf_op jit(solution)/shard_map/all_gather | solution.py:154
  99.7 8.0 %all-gather.21.cloned.1.call-done = bf16[4,480,528]{1,2,0:T(8,128)(2,1)} async-done(((bf16[1,480,528]{1,2,0:T(8,128)(2,1)}), bf16[4,480,528]{1,2,0:T(8,128)(2,1)}) %all-gather.21.cloned.1.call-update) | async-done | bytes 2027536 | tf_op jit(solution)/shard_map/all_gather | solution.py:48
  107.7 3.3 copy.49
  111.0 3.4 reshape.240
  114.4 1.5 slice_convert_fusion
  115.9 2.4 fusion.58
  118.3 2.5 copy.50
  120.8 2.4 subtract_convert_fusion
  123.4 2.4 copy.54
  125.7 1.9 multiply_subtract_fusion
  127.7 0.8 copy.52
  128.5 4.2 fusion.59
  132.8 5.8 %fusion.8 = (bf16[132,5,4]{0,2,1:T(4,128)(2,1)S(1)}, f32[5,528,132,4]{1,2,3,0:T(8,128)}) fusion(pred[132,528]{1,0:T(8,128)(4,1)} %fusion.39, s32[]{:T(128)S(6)} %select_n.30, bf16[528,5,4,32]{0,3,2,1:T(8,128)(2,1)S(1)} %bitcast.113, bf16[528,5,4,32]{0,3,2,1:T(8,128)(2,1)S(1)} %bitcast.114, bf16[528,5,32]{0,2,1:T(8,128)(2,1)} %get-tuple-element.13, ...), kind=kOutput, calls=%fused_computation.12 | convolution fusion | flops 183952560 | bytes 7340260 | tf_op jit(solution)/shard_map/rkgd,jkd->rkgj/dot_general | solution.py:98
  138.9 8.9 %bitcast_reduce_fusion = (bf16[512,5,4]{0,2,1:T(4,128)(2,1)S(1)}, f32[5,512,4,512]{1,3,2,0:T(8,128)}) fusion(pred[512]{0:T(512)(128)(4,1)S(1)} %slice_reduce_fusion, bf16[512,5,4,64]{0,3,2,1:T(8,128)(2,1)S(1)} %bitcast.119, bf16[512,5,64,1]{0,2,3,1:T(8,128)(2,1)S(1)} %bitcast.120), kind=kOutput, calls=%fused_computation.1 | convolution fusion | flops 686807040 | bytes 22630912 | tf_op jit(solution)/shard_map/rkgd,pkd->rkgp/dot_general | solution.py:73
  147.8 16.1 %pmax.7 = bf16[528,5,4]{0,2,1:T(4,128)(2,1)S(1)} all-reduce(bf16[528,5,4]{0,2,1:T(4,128)(2,1)S(1)} %fusion.45), channel_id=1, replica_groups=mesh['tok'=8,'wid'=4] {'wid'}, use_global_device_ids=true, to_apply=%region_4.5 | all-reduce | flops 10560 | bytes 42240 | tf_op jit(solution)/shard_map/pmax | solution.py:106
  163.9 0.7 constant_dynamic-slice_fusion
  164.8 0.6 copy-done.16
  165.4 4.7 %fusion.41 = f32[16,5,4,64]{3,2,1,0:T(4,128)} fusion(bf16[16,512,5,64]{1,3,2,0:T(8,128)(2,1)} %bitcast.111, f32[16,5,4,512]{3,2,1,0:T(4,128)S(1)} %copy-done.2, f32[16,5,4]{2,1,0:T(8,128)S(1)} %copy.56), kind=kOutput, calls=%fused_computation.67 | convolution fusion | flops 21299200 | bytes 5981440 | tf_op jit(solution)/shard_map/jkgp,jpkd->jkgd/dot_general | solution.py:122
  170.1 2.1 copy.57
  172.3 1.0 copy.58
  173.2 9.5 %fusion.14 = f32[512,5,4,64]{0,3,2,1:T(8,128)S(1)} fusion(bf16[512,5,64,1]{0,2,3,1:T(8,128)(2,1)S(1)} %bitcast.123, f32[5,512,4,512]{1,3,2,0:T(8,128)} %get-tuple-element.21, f32[512,5,4]{0,2,1:T(4,128)S(1)} %slice.104, pred[512]{0:T(512)(128)(4,1)S(1)} %slice_reduce_fusion), kind=kOutput, calls=%fused_computation.27 | convolution fusion | flops 692060160 | bytes 23962112 | tf_op jit(solution)/shard_map/rkgp,pkd->rkgd/dot_general | solution.py:116
  182.8 1.4 pad_maximum_fusion
  184.3 2.7 fusion.20
  187.0 6.9 %dynamic_update_slice.10 = bf16[528,5,4,64]{0,3,2,1:T(8,128)(2,1)} dynamic-update-slice(bf16[528,5,4,64]{0,3,2,1:T(8,128)(2,1)} %pad_maximum_fusion, bf16[132,5,4,64]{0,3,2,1:T(8,128)(2,1)S(1)} %fusion.20, s32[]{:T(128)S(6)} %select_n.30, s32[]{:T(128)} %constant.9.clone.1, s32[]{:T(128)} %constant.9.clone.1, s32[]{:T(128)} %constant.9.clone.1) | dynamic-update-slice | bytes 675844 | tf_op jit(solution)/shard_map/dynamic_update_slice | solution.py:137
  193.9 9.9 %fusion.1 = f32[512,5,4]{0,2,1:T(4,128)S(1)} fusion(f32[5,512,4,512]{1,3,2,0:T(8,128)} %get-tuple-element.21, f32[512,5,4]{0,2,1:T(4,128)S(1)} %slice.104, pred[512]{0:T(512)(128)(4,1)S(1)} %copy-done.24), kind=kLoop, calls=%fused_computation.4 | loop fusion | flops 20961280 | bytes 21053952 | tf_op jit(solution)/shard_map/reduce_sum | solution.py:113
  203.8 0.4 fusion.35
  204.4 4.3 fusion.6
  209.1 17.5 %psum.15 = bf16[528,20]{0,1:T(8,128)(2,1)S(1)} all-reduce(bf16[528,20]{0,1:T(8,128)(2,1)S(1)} %convert_element_type.114), channel_id=1, replica_groups=mesh['tok'=8,'wid'=4] {'wid'}, use_global_device_ids=true, to_apply=%region_9.10 | all-reduce | flops 10560 | bytes 42240 | tf_op jit(solution)/shard_map/psum | solution.py:150
  226.6 31.2 %all-reduce.2.cloned.1.call-done = bf16[528,1280]{0,1:T(8,128)(2,1)} async-done(((bf16[528,1280]{0,1:T(8,128)(2,1)}), bf16[528,1280]{0,1:T(8,128)(2,1)}) %all-reduce.2.cloned.1.call-update) | async-done | bytes 1351696 | tf_op jit(solution)/shard_map/psum | solution.py:147
  257.7 1.8 fusion.12
  259.5 0.9 convolution_add_fusion
  260.4 0.9 copy-done.6
  261.3 0.8 convert_bitcast_fusion
  262.2 0.5 all-gather.13.cloned.1.call-update
  262.8 0.7 all-gather.15.cloned.1.call-update
  263.5 0.7 all-gather.17.cloned.1.call-update
  264.2 0.3 reduce-scatter.4.cloned.1.call-start
  264.6 29.2 %all-gather.23.cloned.1.call-done = bf16[4,320,528]{1,2,0:T(8,128)(2,1)} async-done(((bf16[1,320,528]{1,2,0:T(8,128)(2,1)}), bf16[4,320,528]{1,2,0:T(8,128)(2,1)}) %all-gather.23.cloned.1.call-update) | async-done | bytes 1351696 | tf_op jit(solution)/shard_map/all_gather | solution.py:158
  293.7 2.0 copy.60
  295.8 3.0 reshape.244
  298.8 2.2 multiply_reduce_fusion
  301.0 25.0 %all-gather.13.cloned.1.call-done = bf16[1280,896]{1,0:T(8,128)(2,1)} async-done(((bf16[160,896]{1,0:T(8,128)(2,1)}), bf16[1280,896]{1,0:T(8,128)(2,1)}) %all-gather.13.cloned.1.call-update) | async-done | bytes 2293776 | tf_op jit(solution)/shard_map/all_gather | solution.py:161
  326.0 4.5 %fusion.57 = f32[528,896]{1,0:T(8,128)} fusion(bf16[1280,896]{1,0:T(8,128)(2,1)} %all-gather.13.cloned.1.call-done, f32[1280,528]{0,1:T(8,128)S(1)} %copy-done, f32[1280]{0:T(1024)S(1)} %copy-done.27, f32[528]{0:T(1024)S(1)} %add_rsqrt_fusion), kind=kOutput, calls=%fused_computation.100 | convolution fusion | flops 1213132800 | bytes 6896704 | tf_op jit(solution)/shard_map/dot_general | solution.py:164
  330.5 27.3 %all-gather.15.cloned.1.call-done = bf16[1280,896]{1,0:T(8,128)(2,1)} async-done(((bf16[160,896]{1,0:T(8,128)(2,1)}), bf16[1280,896]{1,0:T(8,128)(2,1)}) %all-gather.15.cloned.1.call-update) | async-done | bytes 2293776 | tf_op jit(solution)/shard_map/all_gather | solution.py:162
  357.9 31.9 %all-gather.17.cloned.1.call-done = bf16[896,1280]{0,1:T(8,128)(2,1)} async-done(((bf16[896,160]{0,1:T(8,128)(2,1)}), bf16[896,1280]{0,1:T(8,128)(2,1)}) %all-gather.17.cloned.1.call-update) | async-done | bytes 2293776 | tf_op jit(solution)/shard_map/all_gather | solution.py:167
  389.7 7.2 %fusion.13 = bf16[1280,528]{0,1:T(8,128)(2,1)} fusion(bf16[896,1280]{0,1:T(8,128)(2,1)} %all-gather.17.cloned.1.call-done, f32[528,896]{1,0:T(8,128)} %fusion.57, bf16[1280,896]{1,0:T(8,128)(2,1)} %all-gather.15.cloned.1.call-done, f32[1280,528]{0,1:T(8,128)S(1)} %copy-done, f32[1280]{0:T(1024)S(1)} %copy-done.27, f32[528]{0:T(1024)S(1)} %add_rsqrt_fusion), kind=kOutput, calls=%fused_computation.21 | convolution fusion | flops 2427752448 | bytes 10542144 | tf_op jit(solution)/shard_map/dot_general | solution.py:169
  397.0 2.7 copy.70
  400.0 0.3 fusion.44
  400.3 0.8 copy.62
  401.2 29.5 %reduce-scatter.4.cloned.1.call-done = bf16[320,528]{1,0:T(8,128)(2,1)} async-done(((bf16[1280,528]{1,0:T(8,128)(2,1)}), bf16[320,528]{1,0:T(8,128)(2,1)}) %reduce-scatter.4.cloned.1.call-update) | async-done | bytes 337936
  430.7 1.2 copy.71
  431.9 0.9 fusion.31
  (111 shorter events, 2.3 us)
Async XLA Ops:
  7.2 36.8 %all-gather.19.cloned.1.call-start = ((), (), s32[]{:S(2)}) async-start(), calls=%async_computation.6 | async-start | bytes 2027520 | tf_op jit(solution)/shard_map/all_gather | solution.py:44
  7.9 61.2 %all-gather.11.cloned.1.call-start = ((), (), s32[]{:S(2)}) async-start(), calls=%async_computation.1 | async-start | bytes 1474560 | tf_op jit(solution)/shard_map/all_gather | solution.py:46
  8.6 99.0 %all-gather.21.cloned.1.call-start = ((), (), s32[]{:S(2)}) async-start(), calls=%async_computation.7 | async-start | bytes 2703360 | tf_op jit(solution)/shard_map/all_gather | solution.py:48
  49.0 20.0 %copy-start.1 = (f32[1280,528]{0,1:T(8,128)S(1)}, f32[1280,528]{0,1:T(8,128)}, u32[]{:S(2)}) copy-start(f32[1280,528]{0,1:T(8,128)} %reshape.243) | copy-start | bytes 8110084
  49.0 20.0 %copy-start.26 = (f32[1280]{0:T(1024)S(1)}, f32[1280]{0:T(1024)}, u32[]{:S(2)}) copy-start(f32[1280]{0:T(1024)} %param.17) | copy-start | bytes 15364
  72.2 185.5 %all-reduce.2.cloned.1.call-start = ((), (), s32[]{:S(2)}) async-start(), calls=%async_computation.2 | async-start | bytes 3276800 | tf_op jit(solution)/shard_map/psum | solution.py:147
  72.2 5.5 %slice-start.3 = ((s8[5570560]{0:T(1024)(128)(4,1)}), s8[4194304]{0:T(1024)(128)(4,1)S(1)}, s32[]{:S(2)}) async-start(s8[5570560]{0:T(1024)(128)(4,1)} %bitcast.121), calls=%async_computation.13 | async-start | bytes 8388608
  72.2 5.5 %slice-start.4 = ((s8[5570560]{0:T(1024)(128)(4,1)}), s8[1376256]{0:T(1024)(128)(4,1)S(1)}, s32[]{:S(2)}) async-start(s8[5570560]{0:T(1024)(128)(4,1)} %bitcast.121), calls=%async_computation.14 | async-start | bytes 2752512
  77.7 2.8 copy-start.25
  77.7 4.4 copy-start.20
  80.8 92.4 %copy-start.23 = (pred[512]{0:T(512)(128)(4,1)}, pred[512]{0:T(512)(128)(4,1)S(1)}, u32[]{:S(2)}) copy-start(pred[512]{0:T(512)(128)(4,1)S(1)} %slice_reduce_fusion) | copy-start | bytes 1540
  82.1 38.7 %copy-start.14 = (f32[528,32]{0,1:T(8,128)}, f32[528,32]{0,1:T(8,128)S(1)}, u32[]{:S(2)}) copy-start(f32[528,32]{0,1:T(8,128)S(1)} %get-tuple-element.14) | copy-start | bytes 202756
  82.1 38.7 %copy-start.15 = (f32[528,32]{0,1:T(8,128)}, f32[528,32]{0,1:T(8,128)S(1)}, u32[]{:S(2)}) copy-start(f32[528,32]{0,1:T(8,128)S(1)} %get-tuple-element.15) | copy-start | bytes 202756
  127.7 5.1 %copy-start.9 = (bf16[528,5,32]{0,2,1:T(8,128)(2,1)}, bf16[528,5,32]{0,2,1:T(8,128)(2,1)S(1)}, u32[]{:S(2)}) copy-start(bf16[528,5,32]{0,2,1:T(8,128)(2,1)S(1)} %get-tuple-element.12) | copy-start | bytes 506884
  132.8 6.1 %slice-start.2 = ((bf16[17,512,320]{1,2,0:T(8,128)(2,1)}), bf16[1,512,320]{1,2,0:T(8,128)(2,1)S(1)}, s32[]{:S(2)}) async-start(bf16[17,512,320]{1,2,0:T(8,128)(2,1)} %param.20), calls=%async_computation.12 | async-start | bytes 655360 | tf_op jit(solution)/shard_map/slice | solution.py:74
  138.9 26.5 %copy-start.2 = (f32[16,5,4,512]{3,2,1,0:T(4,128)S(1)}, f32[16,5,4,512]{3,2,1,0:T(4,128)}, u32[]{:S(2)}) copy-start(f32[16,5,4,512]{3,2,1,0:T(4,128)} %get-tuple-element.19) | copy-start | bytes 1966084
  164.8 0.6 copy-start.16
  165.4 6.9 %copy-start.4 = (bf16[528,320]{1,0:T(8,128)(2,1)S(1)}, bf16[528,320]{1,0:T(8,128)(2,1)}, u32[]{:S(2)}) copy-start(bf16[528,320]{1,0:T(8,128)(2,1)} %get-tuple-element.10) | copy-start | bytes 1013764
  165.4 7.9 %slice-start.5 = ((bf16[17,512,320]{1,2,0:T(8,128)(2,1)}), bf16[1,512,320]{1,2,0:T(8,128)(2,1)S(1)}, s32[]{:S(2)}) async-start(bf16[17,512,320]{1,2,0:T(8,128)(2,1)} %param.21), calls=%async_computation.15 | async-start | bytes 655360 | tf_op jit(solution)/shard_map/slice | solution.py:119
  170.1 14.1 %slice-start = ((s8[6963200]{0:T(1024)(128)(4,1)}), s8[2768896]{0:T(1024)(128)(4,1)S(1)}, s32[]{:S(2)}) async-start(s8[6963200]{0:T(1024)(128)(4,1)} %bitcast.109), calls=%async_computation.10 | async-start | bytes 5537792
  173.2 9.5 %copy-start.8 = (f32[16,5,4,64]{0,3,2,1:T(8,128)S(1)}, f32[16,5,4,64]{0,3,2,1:T(8,128)}, u32[]{:S(2)}) copy-start(f32[16,5,4,64]{0,3,2,1:T(8,128)} %copy.57) | copy-start | bytes 245764
  173.2 11.0 %slice-start.1 = ((s8[6963200]{0:T(1024)(128)(4,1)}), s8[4194304]{0:T(1024)(128)(4,1)S(1)}, s32[]{:S(2)}) async-start(s8[6963200]{0:T(1024)(128)(4,1)} %bitcast.109), calls=%async_computation.11 | async-start | bytes 8388608
  182.8 1.5 copy-start.13
  182.8 1.5 copy-start.18
  182.8 1.5 copy-start.21
  187.0 7.0 %copy-start.24 = (pred[512]{0:T(512)(128)(4,1)S(1)}, pred[512]{0:T(512)(128)(4,1)}, u32[]{:S(2)}) copy-start(pred[512]{0:T(512)(128)(4,1)} %copy-done.23) | copy-start | bytes 1540
  193.8 10.0 %copy-start.3 = (f32[16,5,4,512]{3,2,1,0:T(4,128)S(1)}, f32[16,5,4,512]{3,2,1,0:T(4,128)}, u32[]{:S(2)}) copy-start(f32[16,5,4,512]{3,2,1,0:T(4,128)} %get-tuple-element.19) | copy-start | bytes 1966084
  193.9 10.0 %copy-start.17 = (f32[16,5,4]{2,1,0:T(8,128)S(1)}, f32[16,5,4]{2,1,0:T(8,128)}, u32[]{:S(2)}) copy-start(f32[16,5,4]{2,1,0:T(8,128)} %copy-done.16) | copy-start | bytes 3844
  193.9 10.5 %copy-start.22 = (f32[132,5,4]{0,2,1:T(4,128)S(1)}, f32[132,5,4]{0,2,1:T(4,128)}, u32[]{:S(2)}) copy-start(f32[132,5,4]{0,2,1:T(4,128)} %constant_dynamic-slice_fusion) | copy-start | bytes 31684
  193.9 99.8 %all-gather.23.cloned.1.call-start = ((), (), s32[]{:S(2)}) async-start(), calls=%async_computation.8 | async-start | bytes 2027520 | tf_op jit(solution)/shard_map/all_gather | solution.py:158
  208.7 50.8 %copy-start.12 = (bf16[1280,320]{1,0:T(8,128)(2,1)S(1)}, bf16[1280,320]{1,0:T(8,128)(2,1)}, u32[]{:S(2)}) copy-start(bf16[1280,320]{1,0:T(8,128)(2,1)} %all_gather.27) | copy-start | bytes 2457604
  208.7 50.8 %copy-start.19 = (bf16[528,320]{1,0:T(8,128)(2,1)S(1)}, bf16[528,320]{1,0:T(8,128)(2,1)}, u32[]{:S(2)}) copy-start(bf16[528,320]{1,0:T(8,128)(2,1)} %param.11) | copy-start | bytes 1013764
  260.4 0.9 copy-start.6
  262.2 63.8 %all-gather.13.cloned.1.call-start = ((), (), s32[]{:S(2)}) async-start(), calls=%async_computation.3 | async-start | bytes 2580480 | tf_op jit(solution)/shard_map/all_gather | solution.py:161
  262.8 95.1 %all-gather.15.cloned.1.call-start = ((), (), s32[]{:S(2)}) async-start(), calls=%async_computation.4 | async-start | bytes 2580480 | tf_op jit(solution)/shard_map/all_gather | solution.py:162
  263.5 126.2 %all-gather.17.cloned.1.call-start = ((), (), s32[]{:S(2)}) async-start(), calls=%async_computation.5 | async-start | bytes 2580480 | tf_op jit(solution)/shard_map/all_gather | solution.py:167
  264.2 166.5 %reduce-scatter.4.cloned.1.call-start = ((), (), s32[]{:S(2)}) async-start(), calls=%async_computation.9 | async-start | bytes 2048000
  298.8 27.2 %copy-start = (f32[1280,528]{0,1:T(8,128)S(1)}, f32[1280,528]{0,1:T(8,128)}, u32[]{:S(2)}) copy-start(f32[1280,528]{0,1:T(8,128)} %reshape.244) | copy-start | bytes 8110084
  298.8 27.2 %copy-start.27 = (f32[1280]{0:T(1024)S(1)}, f32[1280]{0:T(1024)}, u32[]{:S(2)}) copy-start(f32[1280]{0:T(1024)} %param.18) | copy-start | bytes 15364
  396.9 2.7 copy-start.10
  396.9 2.8 copy-start.11
  396.9 3.0 copy-start.5
  399.7 32.3 %copy-start.7 = (f32[528,320]{1,0:T(8,128)S(1)}, f32[528,320]{1,0:T(8,128)}, u32[]{:S(2)}) copy-start(f32[528,320]{1,0:T(8,128)} %copy-done.6) | copy-start | bytes 2027524
Sparse Core Ops, SparseCore 0:
  9.8 34.0 all-gather.18
  45.6 23.4 all-gather.10
  72.3 35.3 all-gather.20
  194.0 63.6 all-reduce.1
  262.3 31.3 all-gather.22
  295.2 30.7 all-gather.12
  327.6 30.1 all-gather.14
  359.5 30.1 all-gather.16
  399.8 30.8 reduce-scatter.3
where the time goes:
time: 440 us; the launch traced here: 439 us
  waiting for transfers between devices  239 us (54%)
  matrix products  51.6 us (12%)
  blocking collectives  51.1 us (12%)
  local copies, waits for them, and re-layouts  49 us (11%)
  other arithmetic  34.1 us (8%)
  between operations  14.4 us (3%)
    all_gather x1, waiting for transfers between devices, shards(): full_rows = lax.all_gather(hidden, 'wid', axis=1, tiled=True)  35.3 us
    unnamed x10, waiting for transfers between devices  32.9 us
    all_gather x1, waiting for transfers between devices, shards(): down_full = lax.all_gather(w_down, 'tok', axis=1, tiled=True)  31.9 us
    psum x1, waiting for transfers between devices, shards(): lax.psum(sums.reshape(row_count, query_width).astype(jnp.bfloat16), 'wid')  31.2 us
    all_gather x1, waiting for transfers between devices, shards(): middle_full = lax.all_gather(middle, 'wid', axis=1, tiled=True)  29.2 us
    all_gather x1, waiting for transfers between devices, shards(): lax.all_gather(w_up, 'tok', axis=0, tiled=True)  27.3 us
    all_gather x1, waiting for transfers between devices, shards(): lax.all_gather(w_gate, 'tok', axis=0, tiled=True)  25 us
    all_gather x1, waiting for transfers between devices, shards(): tall_cols = lax.all_gather(w_qkv, 'tok', axis=0, tiled=True)  17.8 us
  transfers between devices with their start and end apart: 9, of which 9 were waited for; matrix products, arithmetic and copies ran while one was open for 10% of the time, Pallas kernels for 0%

commit v1 on v0

--- a/solution.py
+++ b/solution.py
@@ -1,6 +1,10 @@
+import functools
+
 import jax
 import jax.numpy as jnp
 from jax import lax
+from jax.experimental import pallas as pl
+from jax.experimental.pallas import tpu as pltpu
 from jax.sharding import PartitionSpec as P
 
 HEADS = 20
@@ -34,7 +38,7 @@
     )
 
 
-def shards(hidden, w_qkv, w_out, w_gate, w_up, w_down, g_attn, g_ffn, lengths, k_cache, v_cache):
+def shards_plain(hidden, w_qkv, w_out, w_gate, w_up, w_down, g_attn, g_ffn, lengths, k_cache, v_cache):
     wid_count = lax.axis_size("wid")
     wid_place = lax.axis_index("wid")
     row_count = hidden.shape[0]
@@ -177,6 +181,420 @@
     return (output, new_kv)
 
 
+MESH = pl.DeviceIdType.MESH
+VMEM_LIMIT = 56 * 1024 * 1024
+
+
+def vmem():
+    return pl.BlockSpec(memory_space=pltpu.VMEM)
+
+
+def params(ident):
+    return pltpu.CompilerParams(
+        collective_id=ident, has_side_effects=True, vmem_limit_bytes=VMEM_LIMIT
+    )
+
+
+def greet(peers):
+    barrier = pltpu.get_barrier_semaphore()
+    for peer in peers:
+        pl.semaphore_signal(barrier, inc=1, device_id=peer, device_id_type=MESH)
+    pl.semaphore_wait(barrier, len(peers))
+
+
+def push(src, dst, send, recv, peer):
+    copy = pltpu.make_async_remote_copy(
+        src_ref=src,
+        dst_ref=dst,
+        send_sem=send,
+        recv_sem=recv,
+        device_id=peer,
+        device_id_type=MESH,
+    )
+    copy.start()
+    return copy
+
+
+def wid_peers(count):
+    tok_place = lax.axis_index("tok")
+    wid_place = lax.axis_index("wid")
+    return [(tok_place, lax.rem(wid_place + k, count)) for k in range(1, count)]
+
+
+def share(src, slots, send, recv, peers, place):
+    return [push(src, slots.at[place], send.at[k], recv.at[k], peer) for k, peer in enumerate(peers)]
+
+
+def mix_kernel(
+    wids, toks, hidden, weight, gain, cosine, sine, turn, out,
+    rows_all, weight_all, mixed_all, wide, send_a, recv_a, send_b, recv_b, send_c, recv_c, send_d, recv_d,
+):
+    wid_place = lax.axis_index("wid")
+    tok_place = lax.axis_index("tok")
+    chips = toks // 2
+    chip = tok_place // 2
+    core = lax.rem(tok_place, 2)
+    peers = wid_peers(wids)
+    line = [(2 * lax.rem(chip + k, chips) + core, wid_place) for k in range(1, chips)]
+    twin = (2 * chip + 1 - core, wid_place)
+    greet(peers + line + [twin])
+    row_copies = share(hidden, rows_all, send_a, recv_a, peers, wid_place)
+    line_copies = share(weight, weight_all, send_b, recv_b, line, tok_place)
+    twin_copies = [push(weight, weight_all.at[tok_place], send_c.at[0], recv_c.at[0], twin)]
+    rows_all[wid_place] = hidden[...]
+    weight_all[tok_place] = weight[...]
+    for k, copy in enumerate(line_copies):
+        copy.wait_recv()
+        source = 2 * lax.rem(chip + chips - k - 1, chips) + core
+        slot = weight_all.at[source]
+        twin_copies.append(push(slot, slot, send_c.at[k + 1], recv_c.at[k + 1], twin))
+    for copy in row_copies:
+        copy.wait_recv()
+    square = 0.0
+    for w in range(wids):
+        part = rows_all[w].astype(jnp.float32)
+        square = square + jnp.sum(part * part, axis=-1, keepdims=True)
+    scale = lax.rsqrt(square * (1.0 / (wids * hidden.shape[1])) + EPSILON)
+    for copy in twin_copies:
+        copy.wait_recv()
+    per = toks // wids
+    total = None
+    for w in range(wids):
+        normed = (rows_all[w].astype(jnp.float32) * scale * gain[w]).astype(jnp.bfloat16)
+        block = weight_all[per * w : per * (w + 1)].reshape(hidden.shape[1], weight.shape[1])
+        term = jnp.dot(normed, block, preferred_element_type=jnp.float32)
+        total = term if total is None else total + term
+    mixed_all[wid_place] = total.astype(jnp.bfloat16)
+    mixed_copies = share(mixed_all.at[wid_place], mixed_all, send_d, recv_d, peers, wid_place)
+    for copy in mixed_copies:
+        copy.wait_recv()
+    width = weight.shape[1]
+    for w in range(wids):
+        wide[:, w * width : (w + 1) * width] = mixed_all[w].astype(jnp.float32)
+    turned = (HEADS + KV_HEADS) * HEAD_DIM
+    for start in range(0, wids * width, 128):
+        part = wide[:, start : start + 128]
+        if start < turned:
+            swapped = jnp.dot(
+                part.astype(jnp.bfloat16), turn[...], preferred_element_type=jnp.float32
+            )
+            spun = part * cosine[...] + swapped * sine[...]
+            if start + 128 > turned:
+                lane = lax.broadcasted_iota(jnp.int32, spun.shape, 1)
+                spun = jnp.where(lane < turned - start, spun, part)
+            part = spun
+        out[:, start : start + 128] = part.astype(jnp.bfloat16)
+    for copy in row_copies + line_copies + twin_copies + mixed_copies:
+        copy.wait_send()
+
+
+def mix(wids, toks, hidden, w_qkv, gain, cosine, sine, turn):
+    rows, width = hidden.shape
+    depth, columns = w_qkv.shape
+    dma = pltpu.SemaphoreType.DMA
+    chips = toks // 2
+    return pl.pallas_call(
+        functools.partial(mix_kernel, wids, toks),
+        out_shape=jax.ShapeDtypeStruct((rows, wids * columns), jnp.bfloat16),
+        in_specs=[vmem()] * 6,
+        out_specs=vmem(),
+        scratch_shapes=[
+            pltpu.VMEM((wids, rows, width), jnp.bfloat16),
+            pltpu.VMEM((toks, depth, columns), jnp.bfloat16),
+            pltpu.VMEM((wids, rows, columns), jnp.bfloat16),
+            pltpu.VMEM((rows, wids * columns), jnp.float32),
+            dma((wids - 1,)), dma((wids - 1,)),
+            dma((chips - 1,)), dma((chips - 1,)),
+            dma((chips,)), dma((chips,)),
+            dma((wids - 1,)), dma((wids - 1,)),
+        ],
+        compiler_params=params(0),
+        cost_estimate=pl.CostEstimate(flops=10**10, bytes_accessed=10**8, transcendentals=0),
+    )(hidden, w_qkv, gain, cosine, sine, turn)
+
+
+def partial_kernel(wids, lengths, mixed, spread, k_old, v_old, sums, stats, dec_sums, dec_stats):
+    place = lax.axis_index("wid")
+    span = k_old.shape[1]
+    fresh = STRETCH // wids
+    query_width = HEADS * HEAD_DIM
+    kv_width = KV_HEADS * HEAD_DIM
+    per = HEADS // wids
+    groups = HEADS // KV_HEADS
+    base = place * span
+    first = pl.multiple_of(place * fresh, fresh)
+    row = lax.broadcasted_iota(jnp.int32, (STRETCH, span + fresh), 0)
+    spot = lax.broadcasted_iota(jnp.int32, (STRETCH, span + fresh), 1)
+    limit = lengths[0] - base
+    seen = ((spot < span) & (spot < limit)) | ((spot >= span) & (spot - span + first <= row))
+    bias = jnp.where(seen, 0.0, MASKED)
+    for g in range(KV_HEADS):
+        at = g * HEAD_DIM
+        keys = jnp.concatenate(
+            [
+                k_old[0, :, at : at + HEAD_DIM],
+                mixed[pl.ds(first, fresh), query_width + at : query_width + at + HEAD_DIM],
+            ],
+            axis=0,
+        )
+        held = query_width + kv_width + at
+        values = jnp.concatenate(
+            [v_old[0, :, at : at + HEAD_DIM], mixed[pl.ds(first, fresh), held : held + HEAD_DIM]],
+            axis=0,
+        )
+        for h in range(g * groups, (g + 1) * groups):
+            query = mixed[:STRETCH, h * HEAD_DIM : (h + 1) * HEAD_DIM] * jnp.bfloat16(SCORE_SCALE)
+            score = (
+                lax.dot_general(
+                    query, keys, (((1,), (1,)), ((), ())), preferred_element_type=jnp.float32
+                )
+                + bias
+            )
+            peak = jnp.max(score, axis=1, keepdims=True)
+            expo = jnp.exp(score - peak)
+            total = jnp.sum(expo, axis=1, keepdims=True)
+            part = jnp.dot(expo.astype(jnp.bfloat16), values, preferred_element_type=jnp.float32)
+            d, i = h // per, h % per
+            sums[d, :, i * HEAD_DIM : (i + 1) * HEAD_DIM] = part.astype(jnp.bfloat16)
+            stats[d, :, i : i + 1] = peak
+            stats[d, :, per + i : per + i + 1] = total
+    rows = spread.shape[1]
+    spots = lax.broadcasted_iota(jnp.int32, (rows, span), 1) + base
+
+    def one(j, carry):
+        query = spread[j]
+        score = (
+            lax.dot_general(
+                query, k_old[j + 1], (((1,), (1,)), ((), ())), preferred_element_type=jnp.float32
+            )
+            * SCORE_SCALE
+        )
+        score = jnp.where(spots < lengths[j + 1], score, MASKED)
+        line = mixed[pl.ds(STRETCH, 16), query_width:].astype(jnp.float32)
+        pick = lax.broadcasted_iota(jnp.int32, line.shape, 0) == j
+        line = jnp.sum(jnp.where(pick, line, 0.0), axis=0, keepdims=True)
+        own = (
+            jnp.sum(query.astype(jnp.float32) * line[:, :kv_width], axis=1, keepdims=True)
+            * SCORE_SCALE
+        )
+        own = jnp.where(place == 0, own, MASKED)
+        peak = jnp.maximum(jnp.max(score, axis=1, keepdims=True), own)
+        expo = jnp.exp(score - peak)
+        expo_own = jnp.exp(own - peak)
+        expo_own = jnp.where(place == 0, expo_own, 0.0)
+        total = jnp.sum(expo, axis=1, keepdims=True) + expo_own
+        part = jnp.dot(
+            expo.astype(jnp.bfloat16), v_old[j + 1], preferred_element_type=jnp.float32
+        )
+        dec_sums[j] = part + expo_own * line[:, kv_width:]
+        dec_stats[j, :, 0:1] = peak
+        dec_stats[j, :, 1:2] = total
+        return carry
+
+    lax.fori_loop(0, k_old.shape[0] - 1, one, 0)
+
+
+def partials(wids, lengths, mixed, spread, k_cache, v_cache):
+    per = HEADS // wids
+    count, rows, width = spread.shape
+    return pl.pallas_call(
+        functools.partial(partial_kernel, wids),
+        out_shape=(
+            jax.ShapeDtypeStruct((wids, STRETCH, per * HEAD_DIM), jnp.bfloat16),
+            jax.ShapeDtypeStruct((wids, STRETCH, 2 * per), jnp.float32),
+            jax.ShapeDtypeStruct((count, rows, width), jnp.float32),
+            jax.ShapeDtypeStruct((count, rows, 2), jnp.float32),
+        ),
+        in_specs=[pl.BlockSpec(memory_space=pltpu.SMEM)] + [vmem()] * 4,
+        out_specs=(vmem(),) * 4,
+        compiler_params=pltpu.CompilerParams(vmem_limit_bytes=VMEM_LIMIT),
+        cost_estimate=pl.CostEstimate(flops=10**10, bytes_accessed=10**8, transcendentals=10**7),
+    )(lengths, mixed, spread, k_cache, v_cache)
+
+
+def swap_kernel(wids, sums, stats, sums_all, stats_all, send_a, recv_a, send_b, recv_b):
+    place = lax.axis_index("wid")
+    peers = wid_peers(wids)
+    greet(peers)
+    copies = []
+    for k, peer in enumerate(peers):
+        copies.append(push(stats.at[peer[1]], stats_all.at[place], send_b.at[k], recv_b.at[k], peer))
+        copies.append(push(sums.at[peer[1]], sums_all.at[place], send_a.at[k], recv_a.at[k], peer))
+    stats_all[place] = stats[place]
+    sums_all[place] = sums[place]
+    for copy in copies:
+        copy.wait()
+
+
+def swap(wids, sums, stats):
+    dma = pltpu.SemaphoreType.DMA
+    return pl.pallas_call(
+        functools.partial(swap_kernel, wids),
+        out_shape=(
+            jax.ShapeDtypeStruct(sums.shape, sums.dtype),
+            jax.ShapeDtypeStruct(stats.shape, stats.dtype),
+        ),
+        in_specs=[vmem()] * 2,
+        out_specs=(vmem(),) * 2,
+        scratch_shapes=[dma((wids - 1,))] * 4,
+        compiler_params=params(1),
+        cost_estimate=pl.CostEstimate(flops=10**10, bytes_accessed=10**8, transcendentals=0),
+    )(sums, stats)
+
+
+def finish_kernel(
+    wids, toks, attended, hidden, w_out, w_gate, w_up, w_down, gain, out,
+    att_all, mid_all, part_all, part_own, residual, active,
+    send_a, recv_a, send_b, recv_b, send_c, recv_c,
+):
+    place = lax.axis_index("wid")
+    peers = wid_peers(wids)
+    greet(peers)
+    width = hidden.shape[1]
+    att_copies = share(attended, att_all, send_a, recv_a, peers, place)
+    att_all[place] = attended[...]
+    for copy in att_copies:
+        copy.wait_recv()
+    total = hidden[...].astype(jnp.float32)
+    for w in range(wids):
+        total = total + jnp.dot(
+            att_all[w], w_out[w * width : (w + 1) * width, :], preferred_element_type=jnp.float32
+        )
+    residual[...] = total
+    mid_all[place] = total.astype(jnp.bfloat16)
+    mid_copies = share(mid_all.at[place], mid_all, send_b, recv_b, peers, place)
+    for copy in mid_copies:
+        copy.wait_recv()
+    square = 0.0
+    for w in range(wids):
+        part = mid_all[w].astype(jnp.float32)
+        square = square + jnp.sum(part * part, axis=-1, keepdims=True)
+    scale = lax.rsqrt(square * (1.0 / (wids * width)) + EPSILON)
+    normed = [
+        (mid_all[w].astype(jnp.float32) * scale * gain[w]).astype(jnp.bfloat16)
+        for w in range(wids)
+    ]
+    hidden_units = w_gate.shape[1]
+    for start in range(0, hidden_units, 128):
+        gate = 0.0
+        up = 0.0
+        for w in range(wids):
+            at = slice(w * width, (w + 1) * width)
+            gate = gate + jnp.dot(
+                normed[w], w_gate[at, start : start + 128], preferred_element_type=jnp.float32
+            )
+            up = up + jnp.dot(
+                normed[w], w_up[at, start : start + 128], preferred_element_type=jnp.float32
+            )
+        active[:, start : start + 128] = (gate / (1.0 + jnp.exp(-gate)) * up).astype(jnp.bfloat16)
+    per = toks // wids
+    narrow = w_down.shape[2]
+    copies = []
+    for k in list(range(1, wids)) + [0]:
+        dest = lax.rem(place + k, wids)
+        for i in range(per):
+            part_own[k, :, i * narrow : (i + 1) * narrow] = jnp.dot(
+                active[...], w_down[dest * per + i], preferred_element_type=jnp.float32
+            ).astype(jnp.bfloat16)
+        if k:
+            copies.append(
+                push(
+                    part_own.at[k], part_all.at[k - 1], send_c.at[k - 1], recv_c.at[k - 1],
+                    peers[k - 1],
+                )
+            )
+    total = residual[...] + part_own[0].astype(jnp.float32)
+    for k, copy in enumerate(copies):
+        copy.wait_recv()
+        total = total + part_all[k].astype(jnp.float32)
+    out[...] = total.astype(jnp.bfloat16)
+    for copy in att_copies + mid_copies + copies:
+        copy.wait_send()
+
+
+def finish(wids, toks, attended, hidden, w_out, w_gate, w_up, w_down, gain):
+    rows, width = hidden.shape
+    dma = pltpu.SemaphoreType.DMA
+    slots = pltpu.VMEM((wids, rows, width), jnp.bfloat16)
+    return pl.pallas_call(
+        functools.partial(finish_kernel, wids, toks),
+        out_shape=jax.ShapeDtypeStruct((rows, width), jnp.bfloat16),
+        in_specs=[vmem()] * 7,
+        out_specs=vmem(),
+        scratch_shapes=[
+            slots,
+            slots,
+            pltpu.VMEM((wids - 1, rows, width), jnp.bfloat16),
+            slots,
+            pltpu.VMEM((rows, width), jnp.float32),
+            pltpu.VMEM((rows, w_gate.shape[1]), jnp.bfloat16),
+        ]
+        + [dma((wids - 1,))] * 6,
+        compiler_params=params(2),
+        cost_estimate=pl.CostEstimate(flops=10**10, bytes_accessed=10**8, transcendentals=0),
+    )(attended, hidden, w_out, w_gate, w_up, w_down, gain)
+
+
+def shards_kernels(hidden, w_qkv, w_out, w_gate, w_up, w_down, g_attn, g_ffn, lengths, k_cache, v_cache):
+    wids = lax.axis_size("wid")
+    toks = lax.axis_size("tok")
+    place = lax.axis_index("wid")
+    rows, width = hidden.shape
+    query_width = HEADS * HEAD_DIM
+    kv_width = KV_HEADS * HEAD_DIM
+    per = HEADS // wids
+    groups = HEADS // KV_HEADS
+    out_whole = lax.all_gather(w_out, "tok", axis=0, tiled=True)
+    gate_whole = lax.all_gather(w_gate, "tok", axis=0, tiled=True)
+    up_whole = lax.all_gather(w_up, "tok", axis=0, tiled=True)
+    down_whole = lax.all_gather(w_down, "tok", axis=0, tiled=False)
+    places = jnp.concatenate([lengths[0] + jnp.arange(STRETCH), lengths[1:]])
+    half = HEAD_DIM // 2
+    ladder = jnp.arange(half).astype(jnp.float32) * (2.0 / HEAD_DIM)
+    freqs = jnp.power(10000.0, -ladder)
+    angles = places.astype(jnp.float32)[:, None] * freqs[None, :]
+    cos, sin = jnp.cos(angles), jnp.sin(angles)
+    cosine = jnp.concatenate([cos, cos, cos, cos], axis=1)
+    sine = jnp.concatenate([-sin, sin, -sin, sin], axis=1)
+    lanes = jnp.arange(128)
+    turn = (lanes[:, None] == (lanes ^ half)[None, :]).astype(jnp.bfloat16)
+    mixed = mix(wids, toks, hidden, w_qkv, g_attn.reshape(wids, 1, width), cosine, sine, turn)
+    share_width = 2 * kv_width // wids
+    new_kv = lax.dynamic_slice_in_dim(mixed, query_width + place * share_width, share_width, 1)
+    count = rows - STRETCH
+    own = mixed[STRETCH:, :query_width].reshape(count, HEADS, 1, HEAD_DIM)
+    member = (jnp.arange(HEADS) // groups)[:, None] == jnp.arange(KV_HEADS)[None, :]
+    spread = jnp.where(member[None, :, :, None], own, jnp.bfloat16(0)).reshape(count, HEADS, kv_width)
+    spread = jnp.pad(spread, ((0, 0), (0, 32 - HEADS), (0, 0)))
+    sums, stats, dec_sums, dec_stats = partials(wids, lengths, mixed, spread, k_cache, v_cache)
+    dec = dec_sums[:, :HEADS].reshape(count, HEADS, KV_HEADS, HEAD_DIM)
+    dec = jnp.where(member[None, :, :, None], dec, 0.0).sum(2).astype(jnp.bfloat16)
+    dec = dec.reshape(count, wids, per * HEAD_DIM).transpose(1, 0, 2)
+    sums = jnp.concatenate([sums, dec], axis=1)
+    dec_stats = dec_stats[:, :HEADS].reshape(count, wids, per, 2).transpose(1, 3, 2, 0)
+    stats = stats.transpose(0, 2, 1)
+    stats = jnp.concatenate([stats, dec_stats.reshape(wids, 2 * per, count)], axis=2)
+    stats = jnp.pad(stats, ((0, 0), (0, 16 - 2 * per), (0, 0)))
+    sums, stats = swap(wids, sums, stats)
+    peaks, totals = stats[:, :per], stats[:, per : 2 * per]
+    weight = jnp.exp(peaks - peaks.max(0, keepdims=True))
+    weight = weight / (weight * totals).sum(0, keepdims=True)
+    weight = jnp.repeat(weight.transpose(0, 2, 1), HEAD_DIM, axis=2)
+    attended = (sums.astype(jnp.float32) * weight).sum(0).astype(jnp.bfloat16)
+    output = finish(
+        wids, toks, attended, hidden, out_whole, gate_whole, up_whole, down_whole,
+        g_ffn.reshape(wids, 1, width),
+    )
+    return (output, new_kv)
+
+
+def shards(*args):
+    wids, toks = lax.axis_size("wid"), lax.axis_size("tok")
+    fits = HEADS % wids == 0 and STRETCH % (128 * wids) == 0 and toks % (2 * wids) == 0
+    fits = fits and args[1].shape[0] % 16 == 0 and args[3].shape[1] % 128 == 0
+    return (shards_kernels if fits else shards_plain)(*args)
+
+
 def solution(mesh):
     placed = (
         P("tok", "wid"),

time: 440 us -> 279 us (0.63)
  waiting for transfers between devices: 239 us -> 2.06 us
  Pallas kernels: 0 us -> 185 us
  matrix products: 51.6 us -> 0 us
  blocking collectives: 51.1 us -> 26.2 us
  other arithmetic: 34.1 us -> 12.8 us
  local copies, waits for them, and re-layouts: 49 us -> 38.4 us
    pallas_call x0 -> x4, Pallas kernels: none -> 185 us  [the longest x1 74.6 us: finish(): pl.pallas_call(functools.partial(finish_kernel, wids, toks), out_shape=ja...]
    all_gather x7 -> x3, waiting for transfers between devices: 175 us -> 0.01 us  [the longest x1 0.01 us: shards_kernels(): down_whole = lax.all_gather(w_down, 'tok', axis=0, tiled=False)]
    dot_general x10 -> x0, matrix products: 51.6 us -> none  [the longest x1 9.5 us: shards(): jnp.einsum('rkgp,pkd->rkgd', expo_stretch.astype(jnp.bfloat16), old_value...]
    psum x1 -> x0, waiting for transfers between devices: 31.2 us -> none  [shards(): lax.psum(sums.reshape(row_count, query_width).astype(jnp.bfloat16), 'wid')]
    unnamed x10 -> x3, waiting for transfers between devices: 32.9 us -> 2.06 us
    psum x1 -> x0, blocking collectives: 17.5 us -> none  [shards(): lax.psum(totals.reshape(row_count, HEADS).astype(jnp.bfloat16), 'wid')]
    pmax x1 -> x0, blocking collectives: 16.1 us -> none  [shards(): lax.pmax(jnp.maximum(cache_peak, fresh_peak).astype(jnp.bfloat16), 'wid')]
    reduce_sum x5 -> x3, other arithmetic: 18.9 us -> 5.26 us  [the longest x1 3.66 us: shards_kernels(): attended = (sums.astype(jnp.float32) * weight).sum(0).astype(jnp.bfloat16)]
  transfers between devices with their start and end apart: 9 -> 3, of which waited for: 9 -> 0; matrix products, arithmetic and copies ran while one was open for 10% -> 18% of each run, Pallas kernels for 0% -> 40%
where the time goes in v1:
time: 279 us; the launch traced here: 278 us
  Pallas kernels  185 us (66%)
  local copies, waits for them, and re-layouts  38.4 us (14%)
  blocking collectives  26.2 us (9%)
  between operations  14 us (5%)
  other arithmetic  12.8 us (5%)
    pallas_call x1, Pallas kernels, finish(): pl.pallas_call(functools.partial(finish_kernel, wids, toks), out_shape=ja...  74.6 us
    pallas_call x1, Pallas kernels, mix(): pl.pallas_call(functools.partial(mix_kernel, wids, toks), out_shape=jax.S...  57.6 us
    pallas_call x1, Pallas kernels, partials(): pl.pallas_call(functools.partial(partial_kernel, wids), out_shape=(jax.Sh...  26.6 us
    all_gather x1, blocking collectives, shards_kernels(): out_whole = lax.all_gather(w_out, 'tok', axis=0, tiled=True)  26.2 us
    pallas_call x1, Pallas kernels, swap(): pl.pallas_call(functools.partial(swap_kernel, wids), out_shape=(jax.Shape...  26 us
    unnamed x12, local copies, waits for them, and re-layouts  20.7 us
  transfers between devices with their start and end apart: 3, of which 0 were waited for; matrix products, arithmetic and copies ran while one was open for 18% of the time, Pallas kernels for 40%

profile of v1, /device:TPU:0, one launch (start us, length us, event | category | flops | bytes accessed | tf_op | source)
XLA Modules:
  0.0 278.4 jit_solution(11233315927096207217)
XLA Ops:
  7.2 0.0 all-gather.9.cloned.1.call-start
  7.2 0.7 all-gather.9.cloned.1.call-update
  7.9 0.0 all-gather.5.cloned.1.call-start
  7.9 0.7 all-gather.5.cloned.1.call-update
  8.6 0.0 all-gather.7.cloned.1.call-start
  8.7 0.7 all-gather.7.cloned.1.call-update
  9.4 0.7 slice.22
  10.1 0.6 iota_add_fusion
  10.8 0.6 fusion.1.turn
  11.4 1.4 reshape.92.gain
  12.8 1.0 fusion
  13.8 1.3 pad_maximum_fusion.1
  15.1 57.6 %shard_map.122.mixed = bf16[528,1920]{1,0:T(8,128)(2,1)} custom-call(bf16[528,320]{1,0:T(8,128)(2,1)} %hidden.3, bf16[160,480]{1,0:T(8,128)(2,1)} %weight.1, f32[4,1,320]{2,1,0:T(1,128)} %reshape.92.gain, f32[528,128]{1,0:T(8,128)} %get-tuple-element.25.cosine, f32[528,128]{1,0:T(8,128)} %get-tuple-element.26.sine, bf16[128,128]{1,0:T(8,128)(2,1)} %fusion.1.turn), custom_call_target="tpu_custom_call" | custom-call | flops 10000000000 | bytes 100000000 | tf_op jit(solution)/shard_map/pallas_call | solution.py:296
  72.7 0.8 slice.23
  73.5 0.1 broadcast_in_dim.56
  73.6 0.1 broadcast_in_dim.57
  73.8 0.4 broadcast_in_dim.58
  74.1 0.1 iota_compare_fusion.2
  74.2 0.1 broadcast_in_dim.53
  74.3 0.1 broadcast_in_dim.54
  74.4 9.0 %copy.50.k_old = bf16[17,512,320]{2,1,0:T(8,128)(2,1)} copy(bf16[17,512,320]{1,2,0:T(8,128)(2,1)} %param.20) | data formatting | bytes 11141120 | tf_op args[9]
  83.4 9.0 %copy.51.v_old = bf16[17,512,320]{2,1,0:T(8,128)(2,1)} copy(bf16[17,512,320]{1,2,0:T(8,128)(2,1)} %param.21) | data formatting | bytes 11141120 | tf_op args[10]
  92.5 0.1 copy_select_fusion
  92.5 0.8 pad.8.spread
  93.3 26.6 %shard_map.123 = (bf16[4,512,320]{2,1,0:T(8,128)(2,1)}, f32[4,512,10]{2,1,0:T(8,128)}, f32[16,32,320]{2,1,0:T(8,128)}, f32[16,32,2]{2,1,0:T(8,128)}) custom-call(s32[17]{0:T(128)} %lengths.1, bf16[528,1920]{1,0:T(8,128)(2,1)} %shard_map.122.mixed, bf16[16,32,320]{2,1,0:T(8,128)(2,1)} %pad.8.spread, bf16[17,512,320]{2,1,0:T(8,128)(2,1)} %copy.50.k_old, ...), custom_call_target="tpu_custom_call" | custom-call | flops 10000000000 | bytes 100000000 | tf_op jit(solution)/shard_map/pallas_call | solution.py:400
  119.9 1.1 slice.24
  121.1 0.0 copy-start.1
  121.1 0.1 copy.52
  121.2 0.2 reshape.93
  121.4 0.0 copy-start
  121.4 0.6 select_reduce_fusion
  122.0 0.1 convert_element_type.38
  122.1 0.0 copy-done.1
  122.2 0.2 copy.56
  122.4 1.6 copy.55
  123.9 0.7 select_maximum_fusion.stats
  124.6 0.0 copy-done
  124.6 1.3 pad_maximum_fusion.sums
  126.0 26.0 %shard_map.124 = (bf16[4,528,320]{2,1,0:T(8,128)(2,1)}, f32[4,16,528]{2,1,0:T(8,128)}) custom-call(bf16[4,528,320]{2,1,0:T(8,128)(2,1)} %pad_maximum_fusion.sums, f32[4,16,528]{2,1,0:T(8,128)} %select_maximum_fusion.stats), custom_call_target="tpu_custom_call" | custom-call | flops 10000000000 | bytes 100000000 | tf_op jit(solution)/shard_map/pallas_call | solution.py:431
  152.0 0.9 slice_reduce_fusion
  152.9 1.0 multiply_reduce_fusion.1
  153.9 0.9 divide_bitcast_fusion
  154.8 0.2 broadcast_in_dim.62
  155.0 0.0 copy-start.3
  155.1 3.2 %copy.59 = f32[4,528,320]{2,1,0:T(8,128)} copy(f32[4,528,320]{1,2,0:T(8,128)S(1)} %bitcast.18) | data formatting | bytes 5406720 | tf_op jit(solution)/shard_map/reshape | solution.py:582
  158.2 0.0 copy-done.3
  158.2 0.7 reshape.97.gain
  158.9 1.1 constant_dynamic-slice_fusion
  160.1 0.8 copy.61
  160.9 0.0 copy-start.2
  160.9 3.7 %multiply_reduce_fusion.attended = bf16[528,320]{1,0:T(8,128)(2,1)} fusion(f32[4,528,320]{2,1,0:T(8,128)} %copy.59, bf16[4,528,320]{2,1,0:T(8,128)(2,1)} %get-tuple-element.12), kind=kLoop, calls=%fused_computation | loop fusion | flops 1858560 | bytes 4392960 | tf_op jit(solution)/shard_map/reduce_sum | solution.py:583
  164.6 0.0 copy-done.2
  164.6 26.2 %all_gather.15.w_out = bf16[1280,320]{1,0:T(8,128)(2,1)} all-gather(bf16[160,320]{1,0:T(8,128)(2,1)S(1)} %copy-done.2), channel_id=1, replica_groups=mesh['tok'=8,'wid'=4] {'tok'}, dimensions={0}, use_global_device_ids=true | all-gather | bytes 921600 | tf_op jit(solution)/shard_map/all_gather | solution.py:547
  190.8 0.0 all-gather.9.cloned.1.call-done
  190.8 4.6 %copy.60 = bf16[7168,160]{1,0:T(8,128)(2,1)} copy(bf16[7168,160]{0,1:T(8,128)(2,1)} %all-gather.9.cloned.1.call-done) | data formatting | bytes 4587520 | tf_op jit(solution)/shard_map/all_gather | solution.py:550
  195.4 0.0 all-gather.5.cloned.1.call-done.w_gate
  195.4 0.0 all-gather.7.cloned.1.call-done.w_up
  195.4 74.6 %shard_map.125 = bf16[528,320]{1,0:T(8,128)(2,1)} custom-call(bf16[528,320]{1,0:T(8,128)(2,1)} %multiply_reduce_fusion.attended, bf16[528,320]{1,0:T(8,128)(2,1)} %hidden.3, bf16[1280,320]{1,0:T(8,128)(2,1)} %all_gather.15.w_out, bf16[1280,896]{1,0:T(8,128)(2,1)} %all-gather.5.cloned.1.call-done.w_gate, bf16[1280,896]{1,0:T(8,128)(2,1)} %all-gather.7.cloned.1.call-done.w_up, ...), custom_call_target="tpu_custom_call" | custom-call | flops 10000000000 | bytes 100000000 | tf_op jit(solution)/shard_map/pallas_call | solution.py:519
  270.1 1.8 copy.66
  (10 shorter events, 0.1 us)
Async XLA Ops:
  7.2 183.6 %all-gather.9.cloned.1.call-start = ((), (), s32[]{:S(2)}) async-start(), calls=%async_computation.2 | async-start | bytes 2580480 | tf_op jit(solution)/shard_map/all_gather | solution.py:550
  7.9 187.5 %all-gather.5.cloned.1.call-start = ((), (), s32[]{:S(2)}) async-start(), calls=%async_computation | async-start | bytes 2580480 | tf_op jit(solution)/shard_map/all_gather | solution.py:548
  8.6 186.8 %all-gather.7.cloned.1.call-start = ((), (), s32[]{:S(2)}) async-start(), calls=%async_computation.1 | async-start | bytes 2580480 | tf_op jit(solution)/shard_map/all_gather | solution.py:549
  121.1 1.1 copy-start.1
  121.4 3.3 %copy-start = (bf16[4,512,320]{2,1,0:T(8,128)(2,1)S(1)}, bf16[4,512,320]{2,1,0:T(8,128)(2,1)}, u32[]{:S(2)}) copy-start(bf16[4,512,320]{2,1,0:T(8,128)(2,1)} %get-tuple-element.8) | copy-start | bytes 3932164
  155.0 3.2 %copy-start.3 = (f32[1280]{0:T(1024)S(1)}, f32[1280]{0:T(1024)}, u32[]{:S(2)}) copy-start(f32[1280]{0:T(1024)} %param.18) | copy-start | bytes 15364
  160.9 3.7 %copy-start.2 = (bf16[160,320]{1,0:T(8,128)(2,1)S(1)}, bf16[160,320]{1,0:T(8,128)(2,1)}, u32[]{:S(2)}) copy-start(bf16[160,320]{1,0:T(8,128)(2,1)} %param.13) | copy-start | bytes 307204
Sparse Core Ops, SparseCore 0:
  9.6 47.6 all-gather.8
  59.0 29.8 all-gather.4
  90.5 30.1 all-gather.6

commit v2 on v1

--- a/solution.py
+++ b/solution.py
@@ -182,6 +182,7 @@
 
 
 MESH = pl.DeviceIdType.MESH
+CHUNKS = 3
 VMEM_LIMIT = 56 * 1024 * 1024
 
 
@@ -221,8 +222,49 @@
     return [(tok_place, lax.rem(wid_place + k, count)) for k in range(1, count)]
 
 
+def cuts(rows):
+    size = rows // CHUNKS
+    return [slice(c * size, (c + 1) * size) for c in range(CHUNKS)]
+
+
+def share_rows(src, slots, at, send, recv, c, peers, place):
+    return [
+        push(src.at[at], slots.at[place, at], send.at[c, k], recv.at[c, k], peer)
+        for k, peer in enumerate(peers)
+    ]
+
+
 def share(src, slots, send, recv, peers, place):
     return [push(src, slots.at[place], send.at[k], recv.at[k], peer) for k, peer in enumerate(peers)]
+
+
+def tok_peers(toks):
+    wid_place = lax.axis_index("wid")
+    tok_place = lax.axis_index("tok")
+    chips = toks // 2
+    chip = tok_place // 2
+    core = lax.rem(tok_place, 2)
+    line = [(2 * lax.rem(chip + k, chips) + core, wid_place) for k in range(1, chips)]
+    return line, (2 * chip + 1 - core, wid_place)
+
+
+def fan(weight, slots, line, twin, send_b, recv_b, send_c, recv_c):
+    tok_place = lax.axis_index("tok")
+    line_copies = share(weight, slots, send_b, recv_b, line, tok_place)
+    twin_copies = [push(weight, slots.at[tok_place], send_c.at[0], recv_c.at[0], twin)]
+    slots[tok_place] = weight[...]
+    return line_copies, twin_copies
+
+
+def relay(slots, line_copies, twin_copies, toks, twin, send_c, recv_c):
+    tok_place = lax.axis_index("tok")
+    chips = toks // 2
+    chip = tok_place // 2
+    core = lax.rem(tok_place, 2)
+    for k, copy in enumerate(line_copies):
+        copy.wait_recv()
+        slot = slots.at[2 * lax.rem(chip + chips - k - 1, chips) + core]
+        twin_copies.append(push(slot, slot, send_c.at[k + 1], recv_c.at[k + 1], twin))
 
 
 def mix_kernel(
@@ -230,61 +272,58 @@
     rows_all, weight_all, mixed_all, wide, send_a, recv_a, send_b, recv_b, send_c, recv_c, send_d, recv_d,
 ):
     wid_place = lax.axis_index("wid")
-    tok_place = lax.axis_index("tok")
-    chips = toks // 2
-    chip = tok_place // 2
-    core = lax.rem(tok_place, 2)
     peers = wid_peers(wids)
-    line = [(2 * lax.rem(chip + k, chips) + core, wid_place) for k in range(1, chips)]
-    twin = (2 * chip + 1 - core, wid_place)
+    line, twin = tok_peers(toks)
     greet(peers + line + [twin])
-    row_copies = share(hidden, rows_all, send_a, recv_a, peers, wid_place)
-    line_copies = share(weight, weight_all, send_b, recv_b, line, tok_place)
-    twin_copies = [push(weight, weight_all.at[tok_place], send_c.at[0], recv_c.at[0], twin)]
+    line_copies, twin_copies = fan(weight, weight_all, line, twin, send_b, recv_b, send_c, recv_c)
+    bands = cuts(hidden.shape[0])
+    row_copies = [
+        share_rows(hidden, rows_all, at, send_a, recv_a, c, peers, wid_place)
+        for c, at in enumerate(bands)
+    ]
     rows_all[wid_place] = hidden[...]
-    weight_all[tok_place] = weight[...]
-    for k, copy in enumerate(line_copies):
-        copy.wait_recv()
-        source = 2 * lax.rem(chip + chips - k - 1, chips) + core
-        slot = weight_all.at[source]
-        twin_copies.append(push(slot, slot, send_c.at[k + 1], recv_c.at[k + 1], twin))
-    for copy in row_copies:
-        copy.wait_recv()
-    square = 0.0
-    for w in range(wids):
-        part = rows_all[w].astype(jnp.float32)
-        square = square + jnp.sum(part * part, axis=-1, keepdims=True)
-    scale = lax.rsqrt(square * (1.0 / (wids * hidden.shape[1])) + EPSILON)
+    relay(weight_all, line_copies, twin_copies, toks, twin, send_c, recv_c)
     for copy in twin_copies:
         copy.wait_recv()
     per = toks // wids
-    total = None
-    for w in range(wids):
-        normed = (rows_all[w].astype(jnp.float32) * scale * gain[w]).astype(jnp.bfloat16)
-        block = weight_all[per * w : per * (w + 1)].reshape(hidden.shape[1], weight.shape[1])
-        term = jnp.dot(normed, block, preferred_element_type=jnp.float32)
-        total = term if total is None else total + term
-    mixed_all[wid_place] = total.astype(jnp.bfloat16)
-    mixed_copies = share(mixed_all.at[wid_place], mixed_all, send_d, recv_d, peers, wid_place)
-    for copy in mixed_copies:
-        copy.wait_recv()
     width = weight.shape[1]
-    for w in range(wids):
-        wide[:, w * width : (w + 1) * width] = mixed_all[w].astype(jnp.float32)
+    mixed_copies = []
+    for c, at in enumerate(bands):
+        for copy in row_copies[c]:
+            copy.wait_recv()
+        square = 0.0
+        for w in range(wids):
+            part = rows_all[w, at].astype(jnp.float32)
+            square = square + jnp.sum(part * part, axis=-1, keepdims=True)
+        scale = lax.rsqrt(square * (1.0 / (wids * hidden.shape[1])) + EPSILON)
+        total = 0.0
+        for w in range(wids):
+            normed = (rows_all[w, at].astype(jnp.float32) * scale * gain[w]).astype(jnp.bfloat16)
+            block = weight_all[per * w : per * (w + 1)].reshape(hidden.shape[1], width)
+            total = total + jnp.dot(normed, block, preferred_element_type=jnp.float32)
+        mixed_all[wid_place, at] = total.astype(jnp.bfloat16)
+        mixed_copies.append(
+            share_rows(mixed_all.at[wid_place], mixed_all, at, send_d, recv_d, c, peers, wid_place)
+        )
     turned = (HEADS + KV_HEADS) * HEAD_DIM
-    for start in range(0, wids * width, 128):
-        part = wide[:, start : start + 128]
-        if start < turned:
-            swapped = jnp.dot(
-                part.astype(jnp.bfloat16), turn[...], preferred_element_type=jnp.float32
-            )
-            spun = part * cosine[...] + swapped * sine[...]
-            if start + 128 > turned:
-                lane = lax.broadcasted_iota(jnp.int32, spun.shape, 1)
-                spun = jnp.where(lane < turned - start, spun, part)
-            part = spun
-        out[:, start : start + 128] = part.astype(jnp.bfloat16)
-    for copy in row_copies + line_copies + twin_copies + mixed_copies:
+    for c, at in enumerate(bands):
+        for copy in mixed_copies[c]:
+            copy.wait_recv()
+        for w in range(wids):
+            wide[at, w * width : (w + 1) * width] = mixed_all[w, at].astype(jnp.float32)
+        for start in range(0, wids * width, 128):
+            part = wide[at, start : start + 128]
+            if start < turned:
+                swapped = jnp.dot(
+                    part.astype(jnp.bfloat16), turn[...], preferred_element_type=jnp.float32
+                )
+                spun = part * cosine[at, :] + swapped * sine[at, :]
+                if start + 128 > turned:
+                    lane = lax.broadcasted_iota(jnp.int32, spun.shape, 1)
+                    spun = jnp.where(lane < turned - start, spun, part)
+                part = spun
+            out[at, start : start + 128] = part.astype(jnp.bfloat16)
+    for copy in sum(row_copies + mixed_copies, line_copies + twin_copies):
         copy.wait_send()
 
 
@@ -303,19 +342,31 @@
             pltpu.VMEM((toks, depth, columns), jnp.bfloat16),
             pltpu.VMEM((wids, rows, columns), jnp.bfloat16),
             pltpu.VMEM((rows, wids * columns), jnp.float32),
-            dma((wids - 1,)), dma((wids - 1,)),
+            dma((CHUNKS, wids - 1)), dma((CHUNKS, wids - 1)),
             dma((chips - 1,)), dma((chips - 1,)),
             dma((chips,)), dma((chips,)),
-            dma((wids - 1,)), dma((wids - 1,)),
+            dma((CHUNKS, wids - 1)), dma((CHUNKS, wids - 1)),
         ],
         compiler_params=params(0),
         cost_estimate=pl.CostEstimate(flops=10**10, bytes_accessed=10**8, transcendentals=0),
     )(hidden, w_qkv, gain, cosine, sine, turn)
 
 
-def partial_kernel(wids, lengths, mixed, spread, k_old, v_old, sums, stats, dec_sums, dec_stats):
+def across(one, other):
+    return lax.dot_general(
+        one, other, (((1,), (1,)), ((), ())), preferred_element_type=jnp.float32
+    )
+
+
+def flip(values):
+    return values.astype(jnp.float32).T.astype(jnp.bfloat16)
+
+
+def partial_kernel(
+    wids, lengths, mixed, spread, k_old, v_old, sums, stats, dec_sums, dec_stats, tall
+):
     place = lax.axis_index("wid")
-    span = k_old.shape[1]
+    span = k_old.shape[2]
     fresh = STRETCH // wids
     query_width = HEADS * HEAD_DIM
     kv_width = KV_HEADS * HEAD_DIM
@@ -323,52 +374,41 @@
     groups = HEADS // KV_HEADS
     base = place * span
     first = pl.multiple_of(place * fresh, fresh)
-    row = lax.broadcasted_iota(jnp.int32, (STRETCH, span + fresh), 0)
-    spot = lax.broadcasted_iota(jnp.int32, (STRETCH, span + fresh), 1)
+    row = lax.broadcasted_iota(jnp.int32, (span + fresh, STRETCH), 1)
+    spot = lax.broadcasted_iota(jnp.int32, (span + fresh, STRETCH), 0)
     limit = lengths[0] - base
     seen = ((spot < span) & (spot < limit)) | ((spot >= span) & (spot - span + first <= row))
     bias = jnp.where(seen, 0.0, MASKED)
     for g in range(KV_HEADS):
         at = g * HEAD_DIM
-        keys = jnp.concatenate(
-            [
-                k_old[0, :, at : at + HEAD_DIM],
-                mixed[pl.ds(first, fresh), query_width + at : query_width + at + HEAD_DIM],
-            ],
-            axis=0,
-        )
         held = query_width + kv_width + at
-        values = jnp.concatenate(
-            [v_old[0, :, at : at + HEAD_DIM], mixed[pl.ds(first, fresh), held : held + HEAD_DIM]],
-            axis=0,
-        )
+        new_keys = mixed[pl.ds(first, fresh), query_width + at : query_width + at + HEAD_DIM]
+        new_values = mixed[pl.ds(first, fresh), held : held + HEAD_DIM]
+        keys = jnp.concatenate([flip(k_old[0, at : at + HEAD_DIM, :]), new_keys], axis=0)
+        values = jnp.concatenate([v_old[0, at : at + HEAD_DIM, :], flip(new_values)], axis=1)
         for h in range(g * groups, (g + 1) * groups):
             query = mixed[:STRETCH, h * HEAD_DIM : (h + 1) * HEAD_DIM] * jnp.bfloat16(SCORE_SCALE)
-            score = (
-                lax.dot_general(
-                    query, keys, (((1,), (1,)), ((), ())), preferred_element_type=jnp.float32
-                )
-                + bias
+            score = across(keys, query) + bias
+            peak = jnp.max(score, axis=0, keepdims=True)
+            expo = jnp.exp(score - peak)
+            total = jnp.sum(expo, axis=0, keepdims=True)
+            tall[h * HEAD_DIM : (h + 1) * HEAD_DIM, :] = jnp.dot(
+                values, expo.astype(jnp.bfloat16), preferred_element_type=jnp.float32
             )
-            peak = jnp.max(score, axis=1, keepdims=True)
-            expo = jnp.exp(score - peak)
-            total = jnp.sum(expo, axis=1, keepdims=True)
-            part = jnp.dot(expo.astype(jnp.bfloat16), values, preferred_element_type=jnp.float32)
             d, i = h // per, h % per
-            sums[d, :, i * HEAD_DIM : (i + 1) * HEAD_DIM] = part.astype(jnp.bfloat16)
-            stats[d, :, i : i + 1] = peak
-            stats[d, :, per + i : per + i + 1] = total
+            stats[d, i : i + 1, :] = peak
+            stats[d, 8 + i : 9 + i, :] = total
+    for d in range(wids):
+        sums[d] = tall[d * per * HEAD_DIM : (d + 1) * per * HEAD_DIM, :].T.astype(jnp.bfloat16)
+        for i in range(per, 8):
+            stats[d, i : i + 1, :] = jnp.ones((1, STRETCH), jnp.float32)
+            stats[d, 8 + i : 9 + i, :] = jnp.ones((1, STRETCH), jnp.float32)
     rows = spread.shape[1]
     spots = lax.broadcasted_iota(jnp.int32, (rows, span), 1) + base
 
     def one(j, carry):
         query = spread[j]
-        score = (
-            lax.dot_general(
-                query, k_old[j + 1], (((1,), (1,)), ((), ())), preferred_element_type=jnp.float32
-            )
-            * SCORE_SCALE
-        )
+        score = jnp.dot(query, k_old[j + 1], preferred_element_type=jnp.float32) * SCORE_SCALE
         score = jnp.where(spots < lengths[j + 1], score, MASKED)
         line = mixed[pl.ds(STRETCH, 16), query_width:].astype(jnp.float32)
         pick = lax.broadcasted_iota(jnp.int32, line.shape, 0) == j
@@ -383,9 +423,7 @@
         expo_own = jnp.exp(own - peak)
         expo_own = jnp.where(place == 0, expo_own, 0.0)
         total = jnp.sum(expo, axis=1, keepdims=True) + expo_own
-        part = jnp.dot(
-            expo.astype(jnp.bfloat16), v_old[j + 1], preferred_element_type=jnp.float32
-        )
+        part = across(expo.astype(jnp.bfloat16), v_old[j + 1])
         dec_sums[j] = part + expo_own * line[:, kv_width:]
         dec_stats[j, :, 0:1] = peak
         dec_stats[j, :, 1:2] = total
@@ -401,138 +439,170 @@
         functools.partial(partial_kernel, wids),
         out_shape=(
             jax.ShapeDtypeStruct((wids, STRETCH, per * HEAD_DIM), jnp.bfloat16),
-            jax.ShapeDtypeStruct((wids, STRETCH, 2 * per), jnp.float32),
+            jax.ShapeDtypeStruct((wids, 16, STRETCH), jnp.float32),
             jax.ShapeDtypeStruct((count, rows, width), jnp.float32),
             jax.ShapeDtypeStruct((count, rows, 2), jnp.float32),
         ),
         in_specs=[pl.BlockSpec(memory_space=pltpu.SMEM)] + [vmem()] * 4,
         out_specs=(vmem(),) * 4,
+        scratch_shapes=[pltpu.VMEM((HEADS * HEAD_DIM, STRETCH), jnp.float32)],
         compiler_params=pltpu.CompilerParams(vmem_limit_bytes=VMEM_LIMIT),
         cost_estimate=pl.CostEstimate(flops=10**10, bytes_accessed=10**8, transcendentals=10**7),
     )(lengths, mixed, spread, k_cache, v_cache)
 
 
-def swap_kernel(wids, sums, stats, sums_all, stats_all, send_a, recv_a, send_b, recv_b):
-    place = lax.axis_index("wid")
-    peers = wid_peers(wids)
-    greet(peers)
-    copies = []
-    for k, peer in enumerate(peers):
-        copies.append(push(stats.at[peer[1]], stats_all.at[place], send_b.at[k], recv_b.at[k], peer))
-        copies.append(push(sums.at[peer[1]], sums_all.at[place], send_a.at[k], recv_a.at[k], peer))
-    stats_all[place] = stats[place]
-    sums_all[place] = sums[place]
-    for copy in copies:
-        copy.wait()
-
-
-def swap(wids, sums, stats):
-    dma = pltpu.SemaphoreType.DMA
-    return pl.pallas_call(
-        functools.partial(swap_kernel, wids),
-        out_shape=(
-            jax.ShapeDtypeStruct(sums.shape, sums.dtype),
-            jax.ShapeDtypeStruct(stats.shape, stats.dtype),
-        ),
-        in_specs=[vmem()] * 2,
-        out_specs=(vmem(),) * 2,
-        scratch_shapes=[dma((wids - 1,))] * 4,
-        compiler_params=params(1),
-        cost_estimate=pl.CostEstimate(flops=10**10, bytes_accessed=10**8, transcendentals=0),
-    )(sums, stats)
-
-
 def finish_kernel(
-    wids, toks, attended, hidden, w_out, w_gate, w_up, w_down, gain, out,
-    att_all, mid_all, part_all, part_own, residual, active,
-    send_a, recv_a, send_b, recv_b, send_c, recv_c,
+    wids, toks, sums, stats, hidden, w_out, w_down, w_gate, w_up, gain, spots, out,
+    sums_all, stats_all, att_all, mid_all, part_all, part_own, residual, out_all, down_all, up_all,
+    send_s, recv_s, send_p, recv_p, send_a, recv_a, send_m, recv_m, send_r, recv_r,
+    send_b, recv_b, send_c, recv_c, send_d, recv_d, send_e, recv_e,
+    send_u, recv_u, send_v, recv_v,
 ):
     place = lax.axis_index("wid")
     peers = wid_peers(wids)
-    greet(peers)
-    width = hidden.shape[1]
-    att_copies = share(attended, att_all, send_a, recv_a, peers, place)
-    att_all[place] = attended[...]
-    for copy in att_copies:
+    line, twin = tok_peers(toks)
+    greet(peers + line + [twin])
+    rows, width = hidden.shape
+    bands = cuts(rows)
+    stat_copies = [
+        push(stats.at[peer[1]], stats_all.at[place], send_s.at[k], recv_s.at[k], peer)
+        for k, peer in enumerate(peers)
+    ]
+    sum_copies = [
+        [
+            push(
+                sums.at[peer[1], at], sums_all.at[place, at], send_p.at[c, k], recv_p.at[c, k], peer
+            )
+            for k, peer in enumerate(peers)
+        ]
+        for c, at in enumerate(bands)
+    ]
+    out_line, out_twin = fan(w_out, out_all, line, twin, send_b, recv_b, send_c, recv_c)
+    up_line, up_twin = fan(w_up, up_all, line, twin, send_u, recv_u, send_v, recv_v)
+    down_line, down_twin = fan(w_down, down_all, line, twin, send_d, recv_d, send_e, recv_e)
+    stats_all[place] = stats[place]
+    sums_all[place] = sums[place]
+    for copy in stat_copies:
         copy.wait_recv()
-    total = hidden[...].astype(jnp.float32)
-    for w in range(wids):
-        total = total + jnp.dot(
-            att_all[w], w_out[w * width : (w + 1) * width, :], preferred_element_type=jnp.float32
+    per = HEADS // wids
+    peaks = [stats_all[w, :8, :] for w in range(wids)]
+    totals = [stats_all[w, 8:, :] for w in range(wids)]
+    peak = functools.reduce(jnp.maximum, peaks)
+    factors = [jnp.exp(one - peak) for one in peaks]
+    whole = functools.reduce(jnp.add, [f * t for f, t in zip(factors, totals)])
+    shares = [
+        lax.dot_general(
+            f / whole, spots[...], (((0,), (0,)), ((), ())),
+            precision=lax.Precision.HIGHEST, preferred_element_type=jnp.float32,
         )
-    residual[...] = total
-    mid_all[place] = total.astype(jnp.bfloat16)
-    mid_copies = share(mid_all.at[place], mid_all, send_b, recv_b, peers, place)
-    for copy in mid_copies:
+        for f in factors
+    ]
+    att_copies = []
+    for c, at in enumerate(bands):
+        for copy in sum_copies[c]:
+            copy.wait_recv()
+        total = 0.0
+        for w in range(wids):
+            total = total + sums_all[w, at].astype(jnp.float32) * shares[w][at]
+        att_all[place, at] = total.astype(jnp.bfloat16)
+        att_copies.append(
+            share_rows(att_all.at[place], att_all, at, send_a, recv_a, c, peers, place)
+        )
+    relay(out_all, out_line, out_twin, toks, twin, send_c, recv_c)
+    for copy in out_twin:
         copy.wait_recv()
-    square = 0.0
-    for w in range(wids):
-        part = mid_all[w].astype(jnp.float32)
-        square = square + jnp.sum(part * part, axis=-1, keepdims=True)
-    scale = lax.rsqrt(square * (1.0 / (wids * width)) + EPSILON)
-    normed = [
-        (mid_all[w].astype(jnp.float32) * scale * gain[w]).astype(jnp.bfloat16)
-        for w in range(wids)
-    ]
-    hidden_units = w_gate.shape[1]
-    for start in range(0, hidden_units, 128):
+    ratio = toks // wids
+    mid_copies = []
+    for c, at in enumerate(bands):
+        for copy in att_copies[c]:
+            copy.wait_recv()
+        total = hidden[at, :].astype(jnp.float32)
+        for w in range(wids):
+            block = out_all[ratio * w : ratio * (w + 1)].reshape(width, width)
+            total = total + jnp.dot(att_all[w, at], block, preferred_element_type=jnp.float32)
+        residual[at, :] = total
+        mid_all[place, at] = total.astype(jnp.bfloat16)
+        mid_copies.append(
+            share_rows(mid_all.at[place], mid_all, at, send_m, recv_m, c, peers, place)
+        )
+    relay(up_all, up_line, up_twin, toks, twin, send_v, recv_v)
+    relay(down_all, down_line, down_twin, toks, twin, send_e, recv_e)
+    for copy in up_twin + down_twin:
+        copy.wait_recv()
+    part_copies = []
+    for c, at in enumerate(bands):
+        for copy in mid_copies[c]:
+            copy.wait_recv()
+        square = 0.0
+        for w in range(wids):
+            part = mid_all[w, at].astype(jnp.float32)
+            square = square + jnp.sum(part * part, axis=-1, keepdims=True)
+        scale = lax.rsqrt(square * (1.0 / (wids * width)) + EPSILON)
         gate = 0.0
         up = 0.0
         for w in range(wids):
-            at = slice(w * width, (w + 1) * width)
-            gate = gate + jnp.dot(
-                normed[w], w_gate[at, start : start + 128], preferred_element_type=jnp.float32
-            )
-            up = up + jnp.dot(
-                normed[w], w_up[at, start : start + 128], preferred_element_type=jnp.float32
-            )
-        active[:, start : start + 128] = (gate / (1.0 + jnp.exp(-gate)) * up).astype(jnp.bfloat16)
-    per = toks // wids
-    narrow = w_down.shape[2]
-    copies = []
-    for k in list(range(1, wids)) + [0]:
-        dest = lax.rem(place + k, wids)
-        for i in range(per):
-            part_own[k, :, i * narrow : (i + 1) * narrow] = jnp.dot(
-                active[...], w_down[dest * per + i], preferred_element_type=jnp.float32
-            ).astype(jnp.bfloat16)
-        if k:
-            copies.append(
-                push(
-                    part_own.at[k], part_all.at[k - 1], send_c.at[k - 1], recv_c.at[k - 1],
-                    peers[k - 1],
+            normed = (mid_all[w, at].astype(jnp.float32) * scale * gain[w]).astype(jnp.bfloat16)
+            deep = slice(w * width, (w + 1) * width)
+            gate = gate + jnp.dot(normed, w_gate[deep, :], preferred_element_type=jnp.float32)
+            block = up_all[ratio * w : ratio * (w + 1)].reshape(width, w_up.shape[1])
+            up = up + jnp.dot(normed, block, preferred_element_type=jnp.float32)
+        active = (gate / (1.0 + jnp.exp(-gate)) * up).astype(jnp.bfloat16)
+        sent = []
+        for k in list(range(1, wids)) + [0]:
+            dest = lax.rem(place + k, wids)
+            block = down_all[pl.ds(dest * ratio, ratio)].reshape(width, w_down.shape[1])
+            term = across(active, block)
+            if k:
+                part_own[k - 1, at] = term.astype(jnp.bfloat16)
+                sent.append(
+                    push(
+                        part_own.at[k - 1, at], part_all.at[k - 1, at],
+                        send_r.at[c, k - 1], recv_r.at[c, k - 1], peers[k - 1],
+                    )
                 )
-            )
-    total = residual[...] + part_own[0].astype(jnp.float32)
-    for k, copy in enumerate(copies):
-        copy.wait_recv()
-        total = total + part_all[k].astype(jnp.float32)
-    out[...] = total.astype(jnp.bfloat16)
-    for copy in att_copies + mid_copies + copies:
+            else:
+                residual[at, :] = residual[at, :] + term
+        part_copies.append(sent)
+    for c, at in enumerate(bands):
+        total = residual[at, :]
+        for k, copy in enumerate(part_copies[c]):
+            copy.wait_recv()
+            total = total + part_all[k, at].astype(jnp.float32)
+        out[at, :] = total.astype(jnp.bfloat16)
+    singles = stat_copies + out_line + out_twin + up_line + up_twin + down_line + down_twin
+    for copy in sum(sum_copies + att_copies + mid_copies + part_copies, singles):
         copy.wait_send()
 
 
-def finish(wids, toks, attended, hidden, w_out, w_gate, w_up, w_down, gain):
+def finish(wids, toks, sums, stats, hidden, w_out, w_down, w_gate, w_up, gain, spots):
     rows, width = hidden.shape
     dma = pltpu.SemaphoreType.DMA
+    chips = toks // 2
     slots = pltpu.VMEM((wids, rows, width), jnp.bfloat16)
+    fewer = pltpu.VMEM((wids - 1, rows, width), jnp.bfloat16)
     return pl.pallas_call(
         functools.partial(finish_kernel, wids, toks),
         out_shape=jax.ShapeDtypeStruct((rows, width), jnp.bfloat16),
-        in_specs=[vmem()] * 7,
+        in_specs=[vmem()] * 9,
         out_specs=vmem(),
         scratch_shapes=[
             slots,
+            pltpu.VMEM(stats.shape, jnp.float32),
             slots,
-            pltpu.VMEM((wids - 1, rows, width), jnp.bfloat16),
             slots,
+            fewer,
+            fewer,
             pltpu.VMEM((rows, width), jnp.float32),
-            pltpu.VMEM((rows, w_gate.shape[1]), jnp.bfloat16),
+            pltpu.VMEM((toks,) + w_out.shape, jnp.bfloat16),
+            pltpu.VMEM((toks,) + w_down.shape, jnp.bfloat16),
+            pltpu.VMEM((toks,) + w_up.shape, jnp.bfloat16),
         ]
-        + [dma((wids - 1,))] * 6,
+        + [dma((wids - 1,))] * 2
+        + [dma((CHUNKS, wids - 1))] * 8
+        + [dma((chips - 1,)), dma((chips - 1,)), dma((chips,)), dma((chips,))] * 3,
         compiler_params=params(2),
         cost_estimate=pl.CostEstimate(flops=10**10, bytes_accessed=10**8, transcendentals=0),
-    )(attended, hidden, w_out, w_gate, w_up, w_down, gain)
+    )(sums, stats, hidden, w_out, w_down, w_gate, w_up, gain, spots)
 
 
 def shards_kernels(hidden, w_qkv, w_out, w_gate, w_up, w_down, g_attn, g_ffn, lengths, k_cache, v_cache):
@@ -544,10 +614,6 @@
     kv_width = KV_HEADS * HEAD_DIM
     per = HEADS // wids
     groups = HEADS // KV_HEADS
-    out_whole = lax.all_gather(w_out, "tok", axis=0, tiled=True)
-    gate_whole = lax.all_gather(w_gate, "tok", axis=0, tiled=True)
-    up_whole = lax.all_gather(w_up, "tok", axis=0, tiled=True)
-    down_whole = lax.all_gather(w_down, "tok", axis=0, tiled=False)
     places = jnp.concatenate([lengths[0] + jnp.arange(STRETCH), lengths[1:]])
     half = HEAD_DIM // 2
     ladder = jnp.arange(half).astype(jnp.float32) * (2.0 / HEAD_DIM)
@@ -559,6 +625,8 @@
     lanes = jnp.arange(128)
     turn = (lanes[:, None] == (lanes ^ half)[None, :]).astype(jnp.bfloat16)
     mixed = mix(wids, toks, hidden, w_qkv, g_attn.reshape(wids, 1, width), cosine, sine, turn)
+    w_gate, mixed = lax.optimization_barrier((w_gate, mixed))
+    gate_whole = lax.all_gather(w_gate, "tok", axis=0, tiled=True)
     share_width = 2 * kv_width // wids
     new_kv = lax.dynamic_slice_in_dim(mixed, query_width + place * share_width, share_width, 1)
     count = rows - STRETCH
@@ -566,24 +634,22 @@
     member = (jnp.arange(HEADS) // groups)[:, None] == jnp.arange(KV_HEADS)[None, :]
     spread = jnp.where(member[None, :, :, None], own, jnp.bfloat16(0)).reshape(count, HEADS, kv_width)
     spread = jnp.pad(spread, ((0, 0), (0, 32 - HEADS), (0, 0)))
-    sums, stats, dec_sums, dec_stats = partials(wids, lengths, mixed, spread, k_cache, v_cache)
+    sums, stats, dec_sums, dec_stats = partials(
+        wids, lengths, mixed, spread, k_cache.transpose(0, 2, 1), v_cache.transpose(0, 2, 1)
+    )
     dec = dec_sums[:, :HEADS].reshape(count, HEADS, KV_HEADS, HEAD_DIM)
     dec = jnp.where(member[None, :, :, None], dec, 0.0).sum(2).astype(jnp.bfloat16)
     dec = dec.reshape(count, wids, per * HEAD_DIM).transpose(1, 0, 2)
     sums = jnp.concatenate([sums, dec], axis=1)
     dec_stats = dec_stats[:, :HEADS].reshape(count, wids, per, 2).transpose(1, 3, 2, 0)
-    stats = stats.transpose(0, 2, 1)
-    stats = jnp.concatenate([stats, dec_stats.reshape(wids, 2 * per, count)], axis=2)
-    stats = jnp.pad(stats, ((0, 0), (0, 16 - 2 * per), (0, 0)))
-    sums, stats = swap(wids, sums, stats)
-    peaks, totals = stats[:, :per], stats[:, per : 2 * per]
-    weight = jnp.exp(peaks - peaks.max(0, keepdims=True))
-    weight = weight / (weight * totals).sum(0, keepdims=True)
-    weight = jnp.repeat(weight.transpose(0, 2, 1), HEAD_DIM, axis=2)
-    attended = (sums.astype(jnp.float32) * weight).sum(0).astype(jnp.bfloat16)
+    dec_stats = jnp.pad(
+        dec_stats, ((0, 0), (0, 0), (0, 8 - per), (0, 0)), constant_values=1.0
+    ).reshape(wids, 16, count)
+    stats = jnp.concatenate([stats, dec_stats], axis=2)
+    lanes_of = (jnp.arange(8)[:, None] == (jnp.arange(width) // HEAD_DIM)[None, :])
     output = finish(
-        wids, toks, attended, hidden, out_whole, gate_whole, up_whole, down_whole,
-        g_ffn.reshape(wids, 1, width),
+        wids, toks, sums, stats, hidden, w_out, w_down.T, gate_whole,
+        w_up, g_ffn.reshape(wids, 1, width), lanes_of.astype(jnp.float32),
     )
     return (output, new_kv)
 
@@ -591,7 +657,7 @@
 def shards(*args):
     wids, toks = lax.axis_size("wid"), lax.axis_size("tok")
     fits = HEADS % wids == 0 and STRETCH % (128 * wids) == 0 and toks % (2 * wids) == 0
-    fits = fits and args[1].shape[0] % 16 == 0 and args[3].shape[1] % 128 == 0
+    fits = fits and args[0].shape[0] % (16 * CHUNKS) == 0 and args[1].shape[0] % 16 == 0 and HEADS // wids <= 8 and args[3].shape[1] % 128 == 0
     return (shards_kernels if fits else shards_plain)(*args)
 
 

time: 279 us -> 198 us (0.71); the launches traced: 278 us -> 195 us
  local copies, waits for them, and re-layouts: 38.4 us -> 10.7 us
  blocking collectives: 26.2 us -> 0 us
  Pallas kernels: 185 us -> 163 us
  other arithmetic: 12.8 us -> 6.94 us
    all_gather x1 -> x0, blocking collectives: 26.2 us -> none  [shards_kernels(): out_whole = lax.all_gather(w_out, 'tok', axis=0, tiled=True)]
    pallas_call x1 -> x0, Pallas kernels: 26 us -> none  [swap(): pl.pallas_call(functools.partial(swap_kernel, wids), out_shape=(jax.Shape...]
    unnamed x12 -> x11, local copies, waits for them, and re-layouts: 20.7 us -> 2.65 us
    pallas_call x1, Pallas kernels: 74.6 us -> 84.1 us  [finish(): pl.pallas_call(functools.partial(finish_kernel, wids, toks), out_shape=ja...]
    pallas_call x1, Pallas kernels: 57.6 us -> 51.2 us  [mix(): pl.pallas_call(functools.partial(mix_kernel, wids, toks), out_shape=jax.S...]
    reduce_sum x2 -> x0, other arithmetic: 4.69 us -> none  [the longest x1 3.66 us: shards_kernels(): attended = (sums.astype(jnp.float32) * weight).sum(0).astype(jnp.bfloat16)]
    all_gather x1 -> x0, local copies, waits for them, and re-layouts: 4.64 us -> none  [shards_kernels(): down_whole = lax.all_gather(w_down, 'tok', axis=0, tiled=False)]
    reshape x2 -> x1, local copies, waits for them, and re-layouts: 3.19 us -> 0.01 us  [shards_kernels(): dec_stats = jnp.pad(dec_stats, ((0, 0), (0, 0), (0, 8 - per), (0, 0)), co...]
  transfers between devices with their start and end apart: 3 -> 1, of which waited for: 0 -> 0; matrix products, arithmetic and copies ran while one was open for 18% -> 5% of each run, Pallas kernels for 40% -> 14%
where the time goes in v2:
time: 198 us; the launch traced here: 195 us
  Pallas kernels  163 us (82%)
  between operations  14.2 us (7%)
  local copies, waits for them, and re-layouts  10.7 us (5%)
  other arithmetic  6.94 us (4%)
    pallas_call x1, Pallas kernels, finish(): pl.pallas_call(functools.partial(finish_kernel, wids, toks), out_shape=ja...  84.1 us
    pallas_call x1, Pallas kernels, mix(): pl.pallas_call(functools.partial(mix_kernel, wids, toks), out_shape=jax.S...  51.2 us
    pallas_call x1, Pallas kernels, partials(): pl.pallas_call(functools.partial(partial_kernel, wids), out_shape=(jax.Sh...  27.3 us
  transfers between devices with their start and end apart: 1, of which 0 were waited for; matrix products, arithmetic and copies ran while one was open for 5% of the time, Pallas kernels for 14%

profile of v2, /device:TPU:0, one launch (start us, length us, event | category | flops | bytes accessed | tf_op | source)
XLA Modules:
  0.0 194.6 jit_solution(13513908881777550279)
XLA Ops:
  7.2 0.0 all-gather.2.cloned.1.call-start
  7.2 0.7 slice.16
  8.0 0.6 iota_add_fusion
  8.6 0.6 fusion.1.turn
  9.2 1.4 reshape.100.gain
  10.6 1.0 fusion
  11.6 1.3 pad_maximum_fusion.1
  12.9 51.2 %shard_map.122.mixed = bf16[528,1920]{1,0:T(8,128)(2,1)} custom-call(bf16[528,320]{1,0:T(8,128)(2,1)} %hidden.3, bf16[160,480]{1,0:T(8,128)(2,1)} %weight.1, f32[4,1,320]{2,1,0:T(1,128)} %reshape.100.gain, f32[528,128]{1,0:T(8,128)} %get-tuple-element.25.cosine, f32[528,128]{1,0:T(8,128)} %get-tuple-element.26.sine, bf16[128,128]{1,0:T(8,128)(2,1)} %fusion.1.turn), custom_call_target="tpu_custom_call" | custom-call | flops 10000000000 | bytes 100000000 | tf_op jit(solution)/shard_map/pallas_call | solution.py:335
  64.1 0.0 all-gather.2.cloned.1.call-update
  64.2 0.8 slice.17
  65.0 0.1 broadcast_in_dim.53
  65.1 0.1 broadcast_in_dim.54
  65.2 0.4 broadcast_in_dim.55
  65.6 0.1 iota_compare_fusion.2
  65.7 0.1 broadcast_in_dim.50
  65.8 0.1 broadcast_in_dim.51
  65.9 0.1 copy_select_fusion
  66.0 0.8 pad.8.spread
  66.8 27.3 %shard_map.123 = (bf16[4,512,320]{2,1,0:T(8,128)(2,1)}, f32[4,16,512]{2,1,0:T(8,128)}, f32[16,32,320]{2,1,0:T(8,128)}, f32[16,32,2]{2,1,0:T(8,128)}) custom-call(s32[17]{0:T(128)} %lengths.1, bf16[528,1920]{1,0:T(8,128)(2,1)} %shard_map.122.mixed, bf16[16,32,320]{2,1,0:T(8,128)(2,1)} %pad.8.spread, bf16[17,320,512]{2,1,0:T(8,128)(2,1)} %bitcast.20, ...), custom_call_target="tpu_custom_call" | custom-call | flops 10000000000 | bytes 100000000 | tf_op jit(solution)/shard_map/pallas_call | solution.py:438
  94.0 1.1 slice.18
  95.1 0.1 copy.33
  95.3 0.0 copy-start.1
  95.3 0.2 reshape.101
  95.5 0.0 copy-start.3
  95.5 0.0 copy-start.2
  95.5 0.0 copy-start
  95.5 0.6 select_reduce_fusion
  96.1 0.1 convert_element_type.33
  96.2 0.0 copy-done.1
  96.3 0.2 copy.36
  96.5 0.0 copy-done.3
  96.5 0.7 reshape.104.gain
  97.2 1.1 constant_dynamic-slice_fusion
  98.3 0.8 copy.38
  99.1 0.0 copy-done.2
  99.2 0.7 pad_maximum_fusion.3.stats
  99.8 0.0 copy-done
  99.8 1.3 pad_maximum_fusion.sums
  101.2 0.6 fusion.2.spots
  101.8 0.0 all-gather.2.cloned.1.call-done.w_gate
  101.8 84.1 %shard_map.124 = bf16[528,320]{1,0:T(8,128)(2,1)} custom-call(bf16[4,528,320]{2,1,0:T(8,128)(2,1)} %pad_maximum_fusion.sums, f32[4,16,528]{2,1,0:T(8,128)} %pad_maximum_fusion.3.stats, bf16[528,320]{1,0:T(8,128)(2,1)} %hidden.3, bf16[160,320]{1,0:T(8,128)(2,1)} %w_out.1, bf16[160,896]{1,0:T(8,128)(2,1)} %bitcast.22, ...), custom_call_target="tpu_custom_call" | custom-call | flops 10000000000 | bytes 100000000 | tf_op jit(solution)/shard_map/pallas_call | solution.py:583
  185.9 1.8 copy.44
  (11 shorter events, 0.1 us)
Async XLA Ops:
  7.2 94.6 %all-gather.2.cloned.1.call-start = ((), (), s32[]{:S(2)}) async-start(), calls=%async_computation | async-start | bytes 2580480 | tf_op jit(solution)/shard_map/all_gather | solution.py:629
  95.3 1.0 copy-start.1
  95.5 1.0 copy-start.3
  95.5 3.7 %copy-start.2 = (f32[4,16,512]{2,1,0:T(8,128)S(1)}, f32[4,16,512]{2,1,0:T(8,128)}, u32[]{:S(2)}) copy-start(f32[4,16,512]{2,1,0:T(8,128)} %get-tuple-element.11) | copy-start | bytes 393220
  95.5 4.3 %copy-start = (bf16[4,512,320]{2,1,0:T(8,128)(2,1)S(1)}, bf16[4,512,320]{2,1,0:T(8,128)(2,1)}, u32[]{:S(2)}) copy-start(bf16[4,512,320]{2,1,0:T(8,128)(2,1)} %get-tuple-element.9) | copy-start | bytes 3932164
Sparse Core Ops, SparseCore 0:
  64.3 29.3 all-gather.1

commit v3 on v2

--- a/solution.py
+++ b/solution.py
@@ -406,13 +406,12 @@
     rows = spread.shape[1]
     spots = lax.broadcasted_iota(jnp.int32, (rows, span), 1) + base
 
-    def one(j, carry):
+    tail = mixed[STRETCH:, query_width:].astype(jnp.float32)
+    for j in range(k_old.shape[0] - 1):
         query = spread[j]
         score = jnp.dot(query, k_old[j + 1], preferred_element_type=jnp.float32) * SCORE_SCALE
         score = jnp.where(spots < lengths[j + 1], score, MASKED)
-        line = mixed[pl.ds(STRETCH, 16), query_width:].astype(jnp.float32)
-        pick = lax.broadcasted_iota(jnp.int32, line.shape, 0) == j
-        line = jnp.sum(jnp.where(pick, line, 0.0), axis=0, keepdims=True)
+        line = tail[j : j + 1]
         own = (
             jnp.sum(query.astype(jnp.float32) * line[:, :kv_width], axis=1, keepdims=True)
             * SCORE_SCALE
@@ -427,9 +426,6 @@
         dec_sums[j] = part + expo_own * line[:, kv_width:]
         dec_stats[j, :, 0:1] = peak
         dec_stats[j, :, 1:2] = total
-        return carry
-
-    lax.fori_loop(0, k_old.shape[0] - 1, one, 0)
 
 
 def partials(wids, lengths, mixed, spread, k_cache, v_cache):

time: 198 us -> 195 us (0.985)
  Pallas kernels: 163 us -> 160 us
    pallas_call x1, Pallas kernels: 27.3 us -> 24.4 us  [partials(): pl.pallas_call(functools.partial(partial_kernel, wids), out_shape=(jax.Sh...]
  transfers between devices with their start and end apart: 1 -> 1, of which waited for: 0 -> 0; matrix products, arithmetic and copies ran while one was open for 5% -> 5% of each run, Pallas kernels for 14% -> 13%
where the time goes in v3:
time: 195 us; the launch traced here: 192 us
  Pallas kernels  160 us (82%)
  between operations  14.2 us (7%)
  local copies, waits for them, and re-layouts  10.7 us (5%)
  other arithmetic  6.94 us (4%)
    pallas_call x1, Pallas kernels, finish(): pl.pallas_call(functools.partial(finish_kernel, wids, toks), out_shape=ja...  84.2 us
    pallas_call x1, Pallas kernels, mix(): pl.pallas_call(functools.partial(mix_kernel, wids, toks), out_shape=jax.S...  51.2 us
    pallas_call x1, Pallas kernels, partials(): pl.pallas_call(functools.partial(partial_kernel, wids), out_shape=(jax.Sh...  24.4 us
  transfers between devices with their start and end apart: 1, of which 0 were waited for; matrix products, arithmetic and copies ran while one was open for 5% of the time, Pallas kernels for 13%

profile of v3, /device:TPU:0, one launch (start us, length us, event | category | flops | bytes accessed | tf_op | source)
XLA Modules:
  0.0 191.7 jit_solution(8034354578158807140)
XLA Ops:
  7.2 0.0 all-gather.2.cloned.1.call-start
  7.2 0.7 slice.16
  8.0 0.6 iota_add_fusion
  8.6 0.6 fusion.1.turn
  9.2 1.4 reshape.100.gain
  10.6 1.0 fusion
  11.6 1.3 pad_maximum_fusion.1
  12.9 51.2 %shard_map.122.mixed = bf16[528,1920]{1,0:T(8,128)(2,1)} custom-call(bf16[528,320]{1,0:T(8,128)(2,1)} %hidden.3, bf16[160,480]{1,0:T(8,128)(2,1)} %weight.1, f32[4,1,320]{2,1,0:T(1,128)} %reshape.100.gain, f32[528,128]{1,0:T(8,128)} %get-tuple-element.25.cosine, f32[528,128]{1,0:T(8,128)} %get-tuple-element.26.sine, bf16[128,128]{1,0:T(8,128)(2,1)} %fusion.1.turn), custom_call_target="tpu_custom_call" | custom-call | flops 10000000000 | bytes 100000000 | tf_op jit(solution)/shard_map/pallas_call | solution.py:335
  64.1 0.0 all-gather.2.cloned.1.call-update
  64.2 0.8 slice.17
  65.0 0.1 broadcast_in_dim.53
  65.1 0.1 broadcast_in_dim.54
  65.2 0.4 broadcast_in_dim.55
  65.6 0.1 iota_compare_fusion.2
  65.7 0.1 broadcast_in_dim.50
  65.8 0.1 broadcast_in_dim.51
  65.9 0.1 copy_select_fusion
  66.0 0.8 pad.8.spread
  66.8 24.4 %shard_map.123 = (bf16[4,512,320]{2,1,0:T(8,128)(2,1)}, f32[4,16,512]{2,1,0:T(8,128)}, f32[16,32,320]{2,1,0:T(8,128)}, f32[16,32,2]{2,1,0:T(8,128)}) custom-call(s32[17]{0:T(128)} %lengths.1, bf16[528,1920]{1,0:T(8,128)(2,1)} %shard_map.122.mixed, bf16[16,32,320]{2,1,0:T(8,128)(2,1)} %pad.8.spread, bf16[17,320,512]{2,1,0:T(8,128)(2,1)} %bitcast.20, ...), custom_call_target="tpu_custom_call" | custom-call | flops 10000000000 | bytes 100000000 | tf_op jit(solution)/shard_map/pallas_call | solution.py:434
  91.1 1.1 slice.18
  92.2 0.1 copy.33
  92.3 0.0 copy-start.1
  92.4 0.2 reshape.101
  92.6 0.0 copy-start.3
  92.6 0.0 copy-start.2
  92.6 0.0 copy-start
  92.6 0.6 select_reduce_fusion
  93.2 0.1 convert_element_type.33
  93.3 0.0 copy-done.1
  93.4 0.2 copy.36
  93.6 0.0 copy-done.3
  93.6 0.7 reshape.104.gain
  94.2 1.1 constant_dynamic-slice_fusion
  95.4 0.8 copy.38
  96.2 0.0 copy-done.2
  96.2 0.7 pad_maximum_fusion.3.stats
  96.9 0.0 copy-done
  96.9 1.3 pad_maximum_fusion.sums
  98.3 0.6 fusion.2.spots
  98.9 0.0 all-gather.2.cloned.1.call-done.w_gate
  98.9 84.2 %shard_map.124 = bf16[528,320]{1,0:T(8,128)(2,1)} custom-call(bf16[4,528,320]{2,1,0:T(8,128)(2,1)} %pad_maximum_fusion.sums, f32[4,16,528]{2,1,0:T(8,128)} %pad_maximum_fusion.3.stats, bf16[528,320]{1,0:T(8,128)(2,1)} %hidden.3, bf16[160,320]{1,0:T(8,128)(2,1)} %w_out.1, bf16[160,896]{1,0:T(8,128)(2,1)} %bitcast.22, ...), custom_call_target="tpu_custom_call" | custom-call | flops 10000000000 | bytes 100000000 | tf_op jit(solution)/shard_map/pallas_call | solution.py:579
  183.1 1.8 copy.44
  (11 shorter events, 0.1 us)
Async XLA Ops:
  7.2 91.7 %all-gather.2.cloned.1.call-start = ((), (), s32[]{:S(2)}) async-start(), calls=%async_computation | async-start | bytes 2580480 | tf_op jit(solution)/shard_map/all_gather | solution.py:625
  92.3 1.0 copy-start.1
  92.6 1.0 copy-start.3
  92.6 3.7 %copy-start.2 = (f32[4,16,512]{2,1,0:T(8,128)S(1)}, f32[4,16,512]{2,1,0:T(8,128)}, u32[]{:S(2)}) copy-start(f32[4,16,512]{2,1,0:T(8,128)} %get-tuple-element.11) | copy-start | bytes 393220
  92.6 4.3 %copy-start = (bf16[4,512,320]{2,1,0:T(8,128)(2,1)S(1)}, bf16[4,512,320]{2,1,0:T(8,128)(2,1)}, u32[]{:S(2)}) copy-start(bf16[4,512,320]{2,1,0:T(8,128)(2,1)} %get-tuple-element.9) | copy-start | bytes 3932164
Sparse Core Ops, SparseCore 0:
  64.3 29.3 all-gather.1
